TPU v7x, 128 devices: a whole 4x4x4 slice. The times are simulated.
128 devices in a mesh: head: 4 (over y), seq: 32 (over x, z, core).
Axes of the slice: x: 4, y: 4, z: 4, core: 2. Of those that a mesh axis runs over, the one named last changes fastest.
Arguments:
- prompts: bfloat16 [64, 256, 4096], P('seq'), may hold values from -6 to 6
- prompt_len: int32 [64], replicated, may hold values from 32 to 256, as said below
- admitted: int32 [4], replicated, may hold values from -1 to 63, as said below
- cache_len: int32 [4], replicated, may hold values from 1024 to 16384, as said below
- cache_kv: bfloat16 [4, 4, 16384, 256], P('head', None, 'seq'), may hold values from -12 to 12
- dec_tokens: bfloat16 [4, 4, 4096], replicated, may hold values from -6 to 6
- w_query: bfloat16 [4096, 4096], P(None, 'head'), may hold values from -0.09375 to 0.09375
- w_key: bfloat16 [4096, 512], P(None, 'head'), may hold values from -0.09375 to 0.09375
- w_value: bfloat16 [4096, 512], P(None, 'head'), may hold values from -0.09375 to 0.09375
- w_out: bfloat16 [4096, 4096], P('head'), may hold values from -0.09375 to 0.09375
- q_gain: float32 [128], replicated, may hold values from 0.25 to 16
- k_gain: float32 [128], replicated, may hold values from 0.25 to 16
Outputs:
- prefill_out: bfloat16 [64, 256, 4096], P('seq', None, 'head')
- handed_kv: bfloat16 [4, 64, 256, 256], P('head', None, 'seq')
- decode_out: bfloat16 [4, 4, 4096], P(None, None, 'head')
Inputs may be any that keep to these rules, and one draw needn't show every extreme that they name: `prompt_len`: some prompt has exactly 256 live tokens. `admitted`: slots with an entry of 0 or more name distinct prompts; in every draw some slot keeps its cache and some slot takes prompt 64 - 1. `cache_len`: some slot has exactly 16384 live positions.
All inputs are finite; a program needn't handle non-finite values.
Results may differ from a plain program's by a relative error of at most 0.02.
The roundings to bfloat16 on the way count: a program that leaves them out, or rounds other values in their place, can miss the bound.
Values may be sent and summed in bfloat16 or wider, within the bound.
A program may use at most 128 MiB of HBM per device.

v0:
```python
import functools

import jax
import jax.numpy as jnp
import numpy as np
from jax import lax
from jax.experimental import pallas as pl
from jax.experimental.pallas import tpu as pltpu
from jax.sharding import PartitionSpec as P

D = 4096
HD = 128
GROUP = 8
WIDTH = GROUP * HD
LP = 256
SLOTS = 4
STEPS = 4
ROWS = SLOTS * STEPS
CACHE = 512
NS = 32
NH = 4
EACH = LP // NS
EPS = 1e-06
THETA = 1000000.0
NEG = -1e30
SCALE = HD ** (-0.5)
LOG2E = 1.4426950408889634
TILE = 256
NT = WIDTH // TILE
F32 = jnp.float32
BF16 = jnp.bfloat16


def dot(a, b):
    return jnp.dot(a, b, preferred_element_type=F32)


def dot_nt(a, b):
    return lax.dot_general(a, b, (((1,), (1,)), ((), ())), preferred_element_type=F32)


def iota(shape, dim):
    return lax.broadcasted_iota(jnp.int32, shape, dim)


def rotation(positions, freq, gain):
    angle = positions.astype(F32) * freq
    sign = jnp.where(iota((1, HD), 1) < HD // 2, -1.0, 1.0)
    return jnp.cos(angle) * gain, jnp.sin(angle) * (pltpu.roll(gain, HD // 2, 1) * sign)


def normrot(a, first, second):
    inverse = lax.rsqrt(jnp.mean(a * a, axis=-1, keepdims=True) + EPS)
    return (a * first + pltpu.roll(a, HD // 2, 1) * second) * inverse


def kernel(
    plen,
    adm,
    clen,
    freq_ref,
    qg_ref,
    kg_ref,
    prompts,
    dec,
    wq,
    wk,
    wv,
    wo,
    cache,
    out,
    handed,
    dec_out,
    x_v,
    wkv_v,
    wq_v,
    wo_v,
    cache_v,
    tab_v,
    kv_v,
    give_v,
    hand_v,
    dq_v,
    dkv_v,
    pa_v,
    part_s,
    part_r,
    own_v,
    out_v,
    soft_s,
    soft_r,
    join_s,
    join_r,
    da_v,
    dpart_s,
    dpart_r,
    dout_v,
    in_sem,
    wq_sem,
    wo_sem,
    out_sem,
    part_ss,
    part_rs,
    seq_ss,
    seq_rs,
    dpart_ss,
    dpart_rs,
):
    y = lax.axis_index("head")
    me = lax.axis_index("seq")
    right = lax.rem(y + 1, NH)
    left = lax.rem(y + NH - 1, NH)

    def remote(src, dst, send, recv, **where):
        return pltpu.make_async_remote_copy(
            src_ref=src,
            dst_ref=dst,
            send_sem=send,
            recv_sem=recv,
            device_id=where,
            device_id_type=pl.DeviceIdType.MESH,
        )

    def rows(start, size):
        return pl.ds(pl.multiple_of(start, size), size)

    load_x0 = pltpu.make_async_copy(prompts.at[0:LP], x_v.at[0:LP], in_sem.at[0])
    load_k = pltpu.make_async_copy(wk, wkv_v.at[:, 0:HD], in_sem.at[1])
    load_v = pltpu.make_async_copy(wv, wkv_v.at[:, HD : 2 * HD], in_sem.at[2])
    load_dec = pltpu.make_async_copy(dec, x_v.at[LP : LP + ROWS], in_sem.at[3])
    load_x1 = pltpu.make_async_copy(
        prompts.at[LP : 2 * LP], x_v.at[LP + ROWS : 2 * LP + ROWS], in_sem.at[4]
    )
    load_cache = pltpu.make_async_copy(cache, cache_v, in_sem.at[5])

    def load_q(j):
        return pltpu.make_async_copy(wq.at[:, j * TILE : (j + 1) * TILE], wq_v.at[j], wq_sem.at[j])

    def load_o(k, j):
        start = lax.rem(y + k, NH) * WIDTH + j * TILE
        return pltpu.make_async_copy(
            wo.at[:, pl.ds(pl.multiple_of(start, TILE), TILE)], wo_v.at[k, j], wo_sem.at[k, j]
        )

    load_x0.start()
    load_k.start()
    load_v.start()
    load_dec.start()
    load_x1.start()
    for j in range(NT):
        load_q(j).start()
    for k in (2, 3, 1, 0):
        for j in range(NT):
            load_o(k, j).start()
    load_cache.start()

    barrier = pltpu.get_barrier_semaphore()

    def greet(i, carry):
        pl.semaphore_signal(
            barrier,
            inc=1,
            device_id={"seq": lax.rem(me + i, NS)},
            device_id_type=pl.DeviceIdType.MESH,
        )
        return carry

    lax.fori_loop(1, NS, greet, 0)
    for k in range(1, NH):
        pl.semaphore_signal(
            barrier,
            inc=1,
            device_id={"head": lax.rem(y + k, NH)},
            device_id_type=pl.DeviceIdType.MESH,
        )

    freq = freq_ref[...]
    q_gain = qg_ref[...]
    k_gain = kg_ref[...]
    spots = iota((LP, HD), 0)
    tab_v[0], tab_v[1] = rotation(spots, freq, q_gain)
    tab_v[2], tab_v[3] = rotation(spots, freq, k_gain)
    admitted = [adm[r] for r in range(SLOTS)]
    handed_len = [plen[jnp.maximum(admitted[r], 0)] for r in range(SLOTS)]
    is_new = [admitted[r] >= 0 for r in range(SLOTS)]
    eff_len = [jnp.where(is_new[r], handed_len[r], clen[r]) for r in range(SLOTS)]

    def per_slot(slot, values):
        picked = jnp.full(slot.shape, values[0], jnp.int32)
        for r in range(1, SLOTS):
            picked = jnp.where(slot == r, values[r], picked)
        return picked

    token = iota((ROWS, HD), 0)
    places = per_slot(token & (SLOTS - 1), eff_len) + (token >> 2)
    dq_first, dq_second = rotation(places, freq, q_gain)
    dk_first, dk_second = rotation(places, freq, k_gain)

    load_x0.wait()
    load_k.wait()
    load_v.wait()
    load_dec.wait()
    kv = dot(x_v[0 : LP + ROWS, :], wkv_v[...])
    kv_v[0:LP, 0:HD] = normrot(kv[0:LP, 0:HD], tab_v[2], tab_v[3]).astype(BF16)
    kv_v[0:LP, HD : 2 * HD] = kv[0:LP, HD : 2 * HD].astype(BF16)
    dkv_v[...] = jnp.zeros_like(dkv_v)
    dkv_v[0:ROWS, 0:HD] = normrot(kv[LP : LP + ROWS, 0:HD], dk_first, dk_second).astype(BF16)
    dkv_v[0:ROWS, HD : 2 * HD] = kv[LP : LP + ROWS, HD : 2 * HD].astype(BF16)
    load_x1.wait()
    kv = dot(x_v[LP + ROWS : 2 * LP + ROWS, :], wkv_v[...])
    kv_v[LP : 2 * LP, 0:HD] = normrot(kv[:, 0:HD], tab_v[2], tab_v[3]).astype(BF16)
    kv_v[LP : 2 * LP, HD : 2 * HD] = kv[:, HD : 2 * HD].astype(BF16)

    place = iota((2 * LP, 2 * LP), 0)
    source = (((place >> 3) & 1) << 8) + ((place & 7) << 5) + (place >> 4)
    pick = jnp.where(source == iota((2 * LP, 2 * LP), 1), 1.0, 0.0).astype(BF16)
    give_v[...] = dot(pick, kv_v[...]).astype(BF16)
    hand_v[rows(me * 16, 16), :] = give_v[rows(me * 16, 16), :]

    pl.semaphore_wait(barrier, NS - 1 + NH - 1)

    def hand(i, way):
        other = lax.rem(me + i, NS)
        return remote(
            give_v.at[rows(other * 16, 16)],
            hand_v.at[rows(way * 16, 16)],
            seq_ss.at[0, other],
            seq_rs.at[0, way],
            seq=other,
        )

    def hand_start(i, carry):
        hand(i, me).start()
        return carry

    lax.fori_loop(1, NS, hand_start, 0)

    order = iota((LP, LP), 0) >= iota((LP, LP), 1)

    def attend(p):
        length = plen[2 * me + p]
        allowed = order & (iota((LP, LP), 1) < length)
        first = 0 if p == 0 else LP + ROWS
        count = LP + ROWS if p == 0 else LP

        def pair(j, carry):
            if p == 0:
                pltpu.make_async_copy(wq.at[:, 0:TILE], wq_v.at[j], wq_sem.at[j]).wait()
            query = dot(x_v[first : first + count, :], wq_v[j])
            parts = []
            for b in range(TILE // HD):
                mine = query[:, b * HD : (b + 1) * HD]
                q_one = normrot(mine[0:LP], tab_v[0], tab_v[1]).astype(BF16)
                if p == 0:
                    new = normrot(mine[LP : LP + ROWS], dq_first, dq_second).astype(BF16)
                    dq_v[rows((j * 2 + b) * ROWS, ROWS), :] = new
                scores = dot_nt(q_one, kv_v[p * LP : (p + 1) * LP, 0:HD])
                scores = jnp.where(allowed, scores, NEG)
                top = jnp.max(scores, axis=-1, keepdims=True)
                expo = jnp.exp2((scores - top) * (SCALE * LOG2E))
                weights = expo * (1.0 / jnp.sum(expo, axis=-1, keepdims=True))
                mixed = dot(weights.astype(BF16), kv_v[p * LP : (p + 1) * LP, HD : 2 * HD])
                parts.append(mixed.astype(BF16))
            pa_v[p, :, rows(j * TILE, TILE)] = jnp.concatenate(parts, axis=1)
            return carry

        lax.fori_loop(0, NT, pair, 0)

    def project(p, k, j):
        return dot(pa_v[p], wo_v[k, j])

    def part(slot, j):
        to = right if slot in (0, 2, 3) else left
        return remote(
            part_s.at[slot, j], part_r.at[slot, j], part_ss.at[slot, j], part_rs.at[slot, j], head=to
        )

    def wait_o(k, j):
        pltpu.make_async_copy(wo.at[:, 0:TILE], wo_v.at[k, j], wo_sem.at[k, j]).wait()

    def send(p, k, slot, far, j, first_use):
        if first_use:
            wait_o(k, j)
        value = project(p, k, j)
        if far is not None:
            part(far, j).wait_recv()
            value = value + part_r[far, j].astype(F32)
        part_s[slot, j] = value.astype(BF16)
        part(slot, j).start()

    attend(0)

    def first_parts(j, carry):
        send(0, 2, 0, None, j, True)
        send(0, 3, 4, None, j, True)
        return carry

    lax.fori_loop(0, NT, first_parts, 0)
    attend(1)

    def second_parts(j, carry):
        send(1, 1, 3, None, j, True)
        send(1, 2, 1, None, j, False)
        return carry

    lax.fori_loop(0, NT, second_parts, 0)

    load_cache.wait()

    def hand_wait(i, carry):
        other = lax.rem(me + i, NS)
        hand(i, other).wait_recv()
        return carry

    lax.fori_loop(1, NS, hand_wait, 0)
    save_hand = pltpu.make_async_copy(hand_v, handed, out_sem.at[0])
    save_hand.start()

    queries = dq_v[...]
    heads = GROUP * ROWS

    def pieces():
        for r in range(SLOTS):
            slot = iota((heads, CACHE), 0) & (SLOTS - 1)
            place = (iota((heads, CACHE), 1) << 5) + me
            limit = jnp.where(is_new[r], 0, clen[r])
            yield (
                dot_nt(queries, cache_v[r * CACHE : (r + 1) * CACHE, 0:HD]),
                (slot == r) & (place < limit),
                cache_v[r * CACHE : (r + 1) * CACHE, HD : 2 * HD],
            )
        slot = iota((heads, 2 * LP), 0) & (SLOTS - 1)
        column = iota((heads, 2 * LP), 1)
        prompt = column >> 3
        place = ((column & 7) << 5) + me
        yield (
            dot_nt(queries, hand_v[:, 0:HD]),
            (prompt == per_slot(slot, admitted)) & (place < per_slot(slot, handed_len)),
            hand_v[:, HD : 2 * HD],
        )
        row = iota((heads, HD), 0)
        column = iota((heads, HD), 1) + jnp.where(me == 0, 0, ROWS)
        yield (
            dot_nt(queries, dkv_v[:, 0:HD]),
            ((row & 3) == (column & 3)) & ((column >> 2) <= ((row >> 2) & 3)) & (column < ROWS),
            dkv_v[:, HD : 2 * HD],
        )

    parts = [(jnp.where(mask, s, NEG), mask, v) for s, mask, v in pieces()]
    top = functools.reduce(jnp.maximum, [jnp.max(s, axis=-1, keepdims=True) for s, _, _ in parts])
    total = jnp.zeros((heads, 1), F32)
    acc = jnp.zeros((heads, HD), F32)
    for s, mask, v in parts:
        expo = jnp.where(mask, jnp.exp2((s - top) * (SCALE * LOG2E)), 0.0)
        total = total + jnp.sum(expo, axis=-1, keepdims=True)
        acc = acc + dot(expo.astype(BF16), v)
    state = jnp.where(iota((heads, HD), 1) < HD // 2, top, total)
    for q in range(heads // NS):
        soft_s[pl.ds(q, NS, stride=8), :] = acc[q * NS : (q + 1) * NS, :]
        soft_s[pl.ds(q + 4, NS, stride=8), :] = state[q * NS : (q + 1) * NS, :]
    soft_r[rows(me * 8, 8), :] = soft_s[rows(me * 8, 8), :]

    def soft(i, way):
        other = lax.rem(me + i, NS)
        return remote(
            soft_s.at[rows(other * 8, 8)],
            soft_r.at[rows(way * 8, 8)],
            seq_ss.at[1, other],
            seq_rs.at[1, way],
            seq=other,
        )

    def soft_start(i, carry):
        soft(i, me).start()
        return carry

    def soft_wait(i, carry):
        soft(i, lax.rem(me + i, NS)).wait_recv()
        return carry

    lax.fori_loop(1, NS, soft_start, 0)

    def own_parts(j, carry):
        wait_o(0, j)
        own_v[0, j] = project(0, 0, j)
        own_v[1, j] = project(1, 0, j)
        return carry

    lax.fori_loop(0, NT, own_parts, 0)

    lax.fori_loop(1, NS, soft_wait, 0)
    joined = []
    for q in range(heads // NS):
        sums = soft_r[pl.ds(q, NS, stride=8), :]
        both = soft_r[pl.ds(q + 4, NS, stride=8), :]
        tops = both[:, 0:1]
        weight = jnp.exp2((tops - jnp.max(tops, axis=0, keepdims=True)) * (SCALE * LOG2E))
        whole = jnp.sum(weight * both[:, HD // 2 : HD // 2 + 1], axis=0, keepdims=True)
        joined.append(jnp.sum(weight * sums, axis=0, keepdims=True) / whole)
    for q in range(heads // NS):
        join_s[q : q + 1, :] = joined[q]
        join_s[q + 4 : q + 5, :] = joined[q]
    join_r[rows(me * 8, 8), :] = join_s[...]

    def join(i, way):
        other = lax.rem(me + i, NS)
        return remote(
            join_s, join_r.at[rows(way * 8, 8)], seq_ss.at[2, other], seq_rs.at[2, way], seq=other
        )

    def join_start(i, carry):
        join(i, me).start()
        return carry

    def join_wait(i, carry):
        join(i, lax.rem(me + i, NS)).wait_recv()
        return carry

    lax.fori_loop(1, NS, join_start, 0)

    def third_parts(j, carry):
        send(0, 1, 2, 0, j, False)
        return carry

    lax.fori_loop(0, NT, third_parts, 0)

    lax.fori_loop(1, NS, join_wait, 0)
    for head in range(GROUP):
        start = (head % 2) * ROWS * 8 + head // 2
        da_v[:, head * HD : (head + 1) * HD] = join_r[pl.ds(start, ROWS, stride=8), :].astype(BF16)

    def dpart(k):
        return remote(
            dpart_s.at[k],
            dpart_r.at[k],
            dpart_ss.at[k],
            dpart_rs.at[k],
            head=lax.rem(y + k, NH),
        )

    def dec_project(k):
        return jnp.concatenate([dot(da_v[...], wo_v[k, j]) for j in range(NT)], axis=1)

    for k in (2, 1, 3):
        dpart_s[k] = dec_project(k).astype(BF16)
        dpart(k).start()
    dec_own = dec_project(0)

    def fourth_parts(j, carry):
        send(1, 3, 5, 1, j, False)
        return carry

    lax.fori_loop(0, NT, fourth_parts, 0)

    for k in (1, 3, 2):
        dpart(k).wait_recv()
        dec_own = dec_own + dpart_r[k].astype(F32)
    dout_v[...] = dec_own.astype(BF16)
    save_dec = pltpu.make_async_copy(dout_v, dec_out, out_sem.at[1])
    save_dec.start()

    def save(p, j):
        return pltpu.make_async_copy(
            out_v.at[p, j], out.at[p * LP : (p + 1) * LP, rows(j * TILE, TILE)], out_sem.at[2 + p]
        )

    def finish(j, carry):
        for p in range(2):
            part(2 + p, j).wait_recv()
            part(4 + p, j).wait_recv()
            value = own_v[p, j] + part_r[2 + p, j].astype(F32) + part_r[4 + p, j].astype(F32)
            out_v[p, j] = value.astype(BF16)
            save(p, j).start()
        return carry

    lax.fori_loop(0, NT, finish, 0)

    def settle(j, carry):
        for slot in range(6):
            part(slot, j).wait_send()
        return carry

    lax.fori_loop(0, NT, settle, 0)

    def settle_seq(i, carry):
        hand(i, me).wait_send()
        soft(i, me).wait_send()
        join(i, me).wait_send()
        return carry

    lax.fori_loop(1, NS, settle_seq, 0)
    for k in range(1, NH):
        dpart(k).wait_send()
    save_hand.wait()
    save_dec.wait()
    for p in range(2):
        pltpu.make_async_copy(
            out.at[p * LP : (p + 1) * LP, :], out.at[p * LP : (p + 1) * LP, :], out_sem.at[2 + p]
        ).wait()


def local(
    prompts,
    prompt_len,
    admitted,
    cache_len,
    cache_kv,
    dec_tokens,
    w_query,
    w_key,
    w_value,
    w_out,
    q_gain,
    k_gain,
):
    half = HD // 2
    one = (THETA ** (-np.arange(half, dtype=np.float64) / half)).astype(np.float32)
    freq = jnp.asarray(np.concatenate([one, one])[None, :])
    smem = pl.BlockSpec(memory_space=pltpu.SMEM)
    vmem = pl.BlockSpec(memory_space=pltpu.VMEM)
    hbm = pl.BlockSpec(memory_space=pl.ANY)
    dma = pltpu.SemaphoreType.DMA
    out, handed, decoded = pl.pallas_call(
        kernel,
        out_shape=[
            jax.ShapeDtypeStruct((2 * LP, WIDTH), BF16),
            jax.ShapeDtypeStruct((2 * LP, 2 * HD), BF16),
            jax.ShapeDtypeStruct((ROWS, WIDTH), BF16),
        ],
        in_specs=[smem] * 3 + [vmem] * 3 + [hbm] * 7,
        out_specs=[hbm] * 3,
        scratch_shapes=[
            pltpu.VMEM((2 * LP + ROWS, D), BF16),
            pltpu.VMEM((D, 2 * HD), BF16),
            pltpu.VMEM((NT, D, TILE), BF16),
            pltpu.VMEM((NH, NT, WIDTH, TILE), BF16),
            pltpu.VMEM((SLOTS * CACHE, 2 * HD), BF16),
            pltpu.VMEM((4, LP, HD), F32),
            pltpu.VMEM((2 * LP, 2 * HD), BF16),
            pltpu.VMEM((2 * LP, 2 * HD), BF16),
            pltpu.VMEM((2 * LP, 2 * HD), BF16),
            pltpu.VMEM((GROUP * ROWS, HD), BF16),
            pltpu.VMEM((HD, 2 * HD), BF16),
            pltpu.VMEM((2, LP, WIDTH), BF16),
            pltpu.VMEM((6, NT, LP, TILE), BF16),
            pltpu.VMEM((6, NT, LP, TILE), BF16),
            pltpu.VMEM((2, NT, LP, TILE), F32),
            pltpu.VMEM((2, NT, LP, TILE), BF16),
            pltpu.VMEM((NS * 8, HD), F32),
            pltpu.VMEM((NS * 8, HD), F32),
            pltpu.VMEM((8, HD), F32),
            pltpu.VMEM((NS * 8, HD), F32),
            pltpu.VMEM((ROWS, WIDTH), BF16),
            pltpu.VMEM((NH, ROWS, WIDTH), BF16),
            pltpu.VMEM((NH, ROWS, WIDTH), BF16),
            pltpu.VMEM((ROWS, WIDTH), BF16),
            dma((6,)),
            dma((NT,)),
            dma((NH, NT)),
            dma((4,)),
            dma((6, NT)),
            dma((6, NT)),
            dma((3, NS)),
            dma((3, NS)),
            dma((NH,)),
            dma((NH,)),
        ],
        compiler_params=pltpu.CompilerParams(
            collective_id=0, has_side_effects=True, vmem_limit_bytes=56 * 2**20
        ),
        cost_estimate=pl.CostEstimate(
            flops=10_500_000_000, bytes_accessed=25_000_000, transcendentals=2_000_000
        ),
    )(
        prompt_len,
        admitted,
        cache_len,
        freq,
        q_gain[None, :],
        k_gain[None, :],
        prompts.reshape(2 * LP, D),
        dec_tokens.reshape(ROWS, D),
        w_query,
        w_key,
        w_value,
        w_out,
        cache_kv.reshape(SLOTS * CACHE, 2 * HD),
    )
    return (
        out.reshape(2, LP, WIDTH),
        handed.reshape(1, 2 * NS, EACH, 2 * HD),
        decoded.reshape(STEPS, SLOTS, WIDTH),
    )


def solution(mesh):
    placed = (
        P("seq", None, None),
        P(),
        P(),
        P(),
        P("head", None, "seq", None),
        P(),
        P(None, "head"),
        P(None, "head"),
        P(None, "head"),
        P("head", None),
        P(),
        P(),
    )
    return jax.shard_map(
        local,
        mesh=mesh,
        in_specs=placed,
        out_specs=(P("seq", None, "head"), P("head", None, "seq", None), P(None, None, "head")),
        check_vma=False,
    )
```

profile of v0, /device:TPU:1, one launch (start us, length us, event | category | flops | bytes accessed | tf_op | source)
XLA Modules:
  0.0 76.5 jit_solution(1284966493652824199)
XLA Ops:
  0.6 1.6 %reshape.25.dec = bf16[16,4096]{1,0:T(8,128)(2,1)} reshape(bf16[4,4,4096]{2,1,0:T(4,128)(2,1)} %param.18) | data formatting | bytes 262144 | tf_op jit(solution)/shard_map/reshape | solution.py:582
  2.2 68.9 %shard_map.148 = (bf16[512,1024]{1,0:T(8,128)(2,1)}, bf16[512,256]{1,0:T(8,128)(2,1)}, bf16[16,1024]{1,0:T(8,128)(2,1)}) custom-call(s32[64]{0:T(128)} %plen.1, s32[4]{0:T(128)} %adm.1, s32[4]{0:T(128)} %clen.1, f32[1,128]{1,0:T(1,128)} %constant.2.clone.freq_ref, f32[1,128]{1,0:T(1,128)} %bitcast.10, f32[1,128]{1,0:T(1,128)} %bitcast.11, ...), custom_call_target="tpu_custom_call" | custom-call | flops 10499999744 | bytes 25000000 | tf_op jit(solution)/shard_map/pallas_call | solution.py:523
  71.1 1.4 %reshape.29 = bf16[4,4,1024]{2,1,0:T(4,128)(2,1)} reshape(bf16[16,1024]{1,0:T(8,128)(2,1)} %get-tuple-element.8) | data formatting | bytes 65536 | tf_op jit(solution)/shard_map/reshape | solution.py:592
  72.5 2.3 %copy.18 = bf16[2,256,1024]{2,1,0:T(8,128)(2,1)} copy(bf16[2,256,1024]{2,1,0:T(8,128)(2,1)} %bitcast.6) | data formatting | bytes 2097152
  74.8 1.7 %copy.19 = bf16[1,64,8,256]{3,2,1,0:T(8,128)(2,1)} copy(bf16[1,64,8,256]{3,2,1,0:T(8,128)(2,1)} %bitcast.7) | data formatting | bytes 524288
where the time goes:
time: 76.7 us; the launch traced here: 76.5 us
  Pallas kernels  68.9 us (90%)
  local copies, waits for them, and re-layouts  6.92 us (9%)
    pallas_call x1, Pallas kernels, local(): pl.pallas_call(kernel, out_shape=[jax.ShapeDtypeStruct((2 * LP, WIDTH), B...  68.9 us
    unnamed x2, local copies, waits for them, and re-layouts  3.93 us
    reshape x1, local copies, waits for them, and re-layouts, local(): dec_tokens.reshape(ROWS, D)  1.59 us

commit v1 on v0

v1 whole, which is shorter than its diff:
```python
import functools

import jax
import jax.numpy as jnp
import numpy as np
from jax import lax
from jax.experimental import pallas as pl
from jax.experimental.pallas import tpu as pltpu
from jax.sharding import PartitionSpec as P

D = 4096
HD = 128
GROUP = 8
WIDTH = GROUP * HD
LP = 256
HALF = LP // 2
SLOTS = 4
STEPS = 4
ROWS = SLOTS * STEPS
CACHE = 512
NS = 32
NH = 4
EACH = LP // NS
EPS = 1e-06
THETA = 1000000.0
NEG = -1e30
SCALE = HD ** (-0.5)
LOG2E = 1.4426950408889634
TILE = 256
NT = WIDTH // TILE
F32 = jnp.float32
BF16 = jnp.bfloat16


def dot(a, b):
    return jnp.dot(a, b, preferred_element_type=F32)


def dot_nt(a, b):
    return lax.dot_general(a, b, (((1,), (1,)), ((), ())), preferred_element_type=F32)


def iota(shape, dim):
    return lax.broadcasted_iota(jnp.int32, shape, dim)


def rotation(positions, freq):
    angle = positions.astype(F32) * freq
    sign = jnp.where(iota((1, HD), 1) < HD // 2, -1.0, 1.0)
    return jnp.cos(angle), jnp.sin(angle) * sign


def gained(cosine, sine, gain):
    return cosine * gain, sine * pltpu.roll(gain, HD // 2, 1)


def normrot(a, first, second):
    inverse = lax.rsqrt(jnp.mean(a * a, axis=-1, keepdims=True) + EPS)
    return (a * first + pltpu.roll(a, HD // 2, 1) * second) * inverse


def kernel(
    plen,
    adm,
    clen,
    freq_ref,
    qg_ref,
    kg_ref,
    prompts,
    dec,
    wq,
    wk,
    wv,
    wo,
    cache,
    out_v,
    hand_v,
    dout_v,
    x_v,
    dec_v,
    wkv_v,
    wq_v,
    wo_v,
    cache_v,
    tab_v,
    kv_v,
    give_v,
    q_v,
    dq_v,
    dkv_v,
    pa_v,
    part_s,
    part_r,
    own_v,
    soft_s,
    soft_r,
    join_s,
    join_r,
    da_v,
    dpart_s,
    dpart_r,
    x_sem,
    in_sem,
    wq_sem,
    wo_sem,
    part_ss,
    part_rs,
    seq_ss,
    seq_rs,
    dpart_ss,
    dpart_rs,
):
    y = lax.axis_index("head")
    me = lax.axis_index("seq")
    right = lax.rem(y + 1, NH)
    left = lax.rem(y + NH - 1, NH)

    def remote(src, dst, send, recv, **where):
        return pltpu.make_async_remote_copy(
            src_ref=src,
            dst_ref=dst,
            send_sem=send,
            recv_sem=recv,
            device_id=where,
            device_id_type=pl.DeviceIdType.MESH,
        )

    def rows(start, size):
        return pl.ds(pl.multiple_of(start, size), size)

    def load_x(half, p):
        source = p * LP + half * HALF
        target = half * (LP + ROWS) + p * HALF
        return pltpu.make_async_copy(
            prompts.at[source : source + HALF], x_v.at[target : target + HALF], x_sem.at[half, p]
        )

    load_k = pltpu.make_async_copy(wk, wkv_v.at[:, 0:HD], in_sem.at[0])
    load_v = pltpu.make_async_copy(wv, wkv_v.at[:, HD : 2 * HD], in_sem.at[1])
    load_dec = pltpu.make_async_copy(dec, dec_v, in_sem.at[2])
    load_cache = pltpu.make_async_copy(cache, cache_v, in_sem.at[3])

    def load_q(j):
        return pltpu.make_async_copy(wq.at[:, j * TILE : (j + 1) * TILE], wq_v.at[j], wq_sem.at[j])

    def load_o(k, j):
        start = lax.rem(y + k, NH) * WIDTH + j * TILE
        return pltpu.make_async_copy(
            wo.at[:, pl.ds(pl.multiple_of(start, TILE), TILE)], wo_v.at[k, j], wo_sem.at[k, j]
        )

    load_dec.start()
    load_k.start()
    load_v.start()
    load_x(0, 0).start()
    load_x(0, 1).start()
    for j in range(NT):
        load_q(j).start()
    for j in range(NT):
        load_o(2, j).start()
        load_o(3, j).start()
    load_x(1, 0).start()
    load_x(1, 1).start()
    for k in (1, 0):
        for j in range(NT):
            load_o(k, j).start()
    load_cache.start()

    barrier = pltpu.get_barrier_semaphore()

    def greet(i, carry):
        pl.semaphore_signal(
            barrier,
            inc=1,
            device_id={"seq": lax.rem(me + i, NS)},
            device_id_type=pl.DeviceIdType.MESH,
        )
        return carry

    for k in range(1, NH):
        pl.semaphore_signal(
            barrier,
            inc=1,
            device_id={"head": lax.rem(y + k, NH)},
            device_id_type=pl.DeviceIdType.MESH,
        )
    lax.fori_loop(1, NS, greet, 0)

    freq = freq_ref[...]
    q_gain = qg_ref[...]
    k_gain = kg_ref[...]
    for half in range(2):
        first, second = rotation(iota((HALF, HD), 0) + half * HALF, freq)
        tab_v[half, 0], tab_v[half, 1] = gained(first, second, q_gain)
        tab_v[half, 2], tab_v[half, 3] = gained(first, second, k_gain)
    admitted = [adm[r] for r in range(SLOTS)]
    handed_len = [plen[jnp.maximum(admitted[r], 0)] for r in range(SLOTS)]
    is_new = [admitted[r] >= 0 for r in range(SLOTS)]
    eff_len = [jnp.where(is_new[r], handed_len[r], clen[r]) for r in range(SLOTS)]

    def per_slot(slot, values):
        picked = jnp.full(slot.shape, values[0], jnp.int32)
        for r in range(1, SLOTS):
            picked = jnp.where(slot == r, values[r], picked)
        return picked

    token = iota((ROWS, HD), 0)
    places = per_slot(token & (SLOTS - 1), eff_len) + (token >> 2)
    first, second = rotation(places, freq)
    dq_first, dq_second = gained(first, second, q_gain)
    dk_first, dk_second = gained(first, second, k_gain)

    load_dec.wait()
    x_v[LP : LP + ROWS, :] = jnp.concatenate(
        [dec_v[t].astype(F32) for t in range(STEPS)], axis=0
    ).astype(BF16)

    def keys_values(half):
        start = half * (LP + ROWS)
        count = LP if half else LP + ROWS
        kv = dot(x_v[start : start + count, :], wkv_v[...])
        for p in range(2):
            mine = kv[p * HALF : (p + 1) * HALF]
            to = slice(p * LP + half * HALF, p * LP + (half + 1) * HALF)
            key = normrot(mine[:, 0:HD], tab_v[half, 2], tab_v[half, 3])
            kv_v[to, 0:HD] = key.astype(BF16)
            kv_v[to, HD : 2 * HD] = mine[:, HD : 2 * HD].astype(BF16)
        if half == 0:
            new = kv[LP : LP + ROWS]
            dkv_v[...] = jnp.zeros_like(dkv_v)
            dkv_v[0:ROWS, 0:HD] = normrot(new[:, 0:HD], dk_first, dk_second).astype(BF16)
            dkv_v[0:ROWS, HD : 2 * HD] = new[:, HD : 2 * HD].astype(BF16)

    def attend(half):
        start = half * (LP + ROWS)
        count = LP if half else LP + ROWS
        for j in range(NT):
            if half == 0:
                load_q(j).wait()
            query = dot(x_v[start : start + count, :], wq_v[j])
            for b in range(TILE // HD):
                head = j * 2 + b
                mine = query[:, b * HD : (b + 1) * HD]
                for p in range(2):
                    one = normrot(mine[p * HALF : (p + 1) * HALF], tab_v[half, 0], tab_v[half, 1])
                    q_v[p, head * HALF : (head + 1) * HALF, :] = one.astype(BF16)
                if half == 0:
                    one = normrot(mine[LP : LP + ROWS], dq_first, dq_second)
                    dq_v[head * ROWS : (head + 1) * ROWS, :] = one.astype(BF16)
        keys = (half + 1) * HALF
        at = iota((keys, HALF), 0)
        causal = at <= iota((keys, HALF), 1) + half * HALF
        for p in range(2):
            bias = jnp.where(causal & (at < plen[2 * me + p]), 0.0, NEG)
            scores = dot_nt(kv_v[p * LP : p * LP + keys, 0:HD], q_v[p])
            scores = scores + jnp.concatenate([bias] * GROUP, axis=1)
            top = jnp.max(scores, axis=0, keepdims=True)
            expo = jnp.exp2((scores - top) * (SCALE * LOG2E))
            weights = expo * (1.0 / jnp.sum(expo, axis=0, keepdims=True))
            values = kv_v[p * LP : p * LP + keys, HD : 2 * HD].astype(F32).T.astype(BF16)
            mixed = dot(values, weights.astype(BF16))
            for head in range(GROUP):
                one = mixed[:, head * HALF : (head + 1) * HALF].T.astype(BF16)
                pa_v[half, p * HALF : (p + 1) * HALF, head * HD : (head + 1) * HD] = one

    def part(slot, j):
        to = right if slot in (0, 2, 3) else left
        return remote(
            part_s.at[slot, j], part_r.at[slot, j], part_ss.at[slot, j], part_rs.at[slot, j], head=to
        )

    def project(half, k, j):
        return dot(pa_v[half], wo_v[k, j])

    def send(half, k, slot, j, far=None, loaded=False):
        if not loaded:
            load_o(k, j).wait()
        value = project(half, k, j)
        if far is not None:
            part(far, j).wait_recv()
            value = value + part_r[far, j].astype(F32)
        part_s[slot, j] = value.astype(BF16)
        part(slot, j).start()

    load_k.wait()
    load_v.wait()
    load_x(0, 0).wait()
    load_x(0, 1).wait()
    keys_values(0)
    attend(0)
    pl.semaphore_wait(barrier, NS - 1 + NH - 1)
    for j in range(NT):
        send(0, 2, 0, j)
        send(0, 3, 4, j)

    load_x(1, 0).wait()
    load_x(1, 1).wait()
    keys_values(1)

    place = iota((2 * LP, 2 * LP), 0)
    source = (((place >> 3) & 1) << 8) + ((place & 7) << 5) + (place >> 4)
    pick = jnp.where(source == iota((2 * LP, 2 * LP), 1), 1.0, 0.0).astype(BF16)
    give_v[...] = dot(pick, kv_v[...]).astype(BF16)
    hand_v[rows(me * 16, 16), :] = give_v[rows(me * 16, 16), :]

    def hand(i, way):
        other = lax.rem(me + i, NS)
        return remote(
            give_v.at[rows(other * 16, 16)],
            hand_v.at[rows(way * 16, 16)],
            seq_ss.at[0, other],
            seq_rs.at[0, way],
            seq=other,
        )

    def hand_start(i, carry):
        hand(i, me).start()
        return carry

    lax.fori_loop(1, NS, hand_start, 0)

    attend(1)
    for j in range(NT):
        send(1, 1, 3, j)
        send(1, 2, 1, j, loaded=True)

    load_cache.wait()

    def hand_wait(i, carry):
        other = lax.rem(me + i, NS)
        hand(i, other).wait_recv()
        return carry

    lax.fori_loop(1, NS, hand_wait, 0)

    queries = dq_v[...]
    heads = GROUP * ROWS

    def pieces():
        for r in range(SLOTS):
            slot = iota((heads, CACHE), 0) & (SLOTS - 1)
            at = (iota((heads, CACHE), 1) << 5) + me
            limit = jnp.where(is_new[r], 0, clen[r])
            yield (
                dot_nt(queries, cache_v[r * CACHE : (r + 1) * CACHE, 0:HD]),
                (slot == r) & (at < limit),
                cache_v[r * CACHE : (r + 1) * CACHE, HD : 2 * HD],
            )
        slot = iota((heads, 2 * LP), 0) & (SLOTS - 1)
        column = iota((heads, 2 * LP), 1)
        prompt = column >> 3
        at = ((column & 7) << 5) + me
        yield (
            dot_nt(queries, hand_v[:, 0:HD]),
            (prompt == per_slot(slot, admitted)) & (at < per_slot(slot, handed_len)),
            hand_v[:, HD : 2 * HD],
        )
        row = iota((heads, HD), 0)
        column = iota((heads, HD), 1) + jnp.where(me == 0, 0, ROWS)
        yield (
            dot_nt(queries, dkv_v[:, 0:HD]),
            ((row & 3) == (column & 3)) & ((column >> 2) <= ((row >> 2) & 3)) & (column < ROWS),
            dkv_v[:, HD : 2 * HD],
        )

    parts = [(jnp.where(mask, s, NEG), mask, v) for s, mask, v in pieces()]
    top = functools.reduce(jnp.maximum, [jnp.max(s, axis=-1, keepdims=True) for s, _, _ in parts])
    total = jnp.zeros((heads, 1), F32)
    acc = jnp.zeros((heads, HD), F32)
    for s, mask, v in parts:
        expo = jnp.where(mask, jnp.exp2((s - top) * (SCALE * LOG2E)), 0.0)
        total = total + jnp.sum(expo, axis=-1, keepdims=True)
        acc = acc + dot(expo.astype(BF16), v)
    state = jnp.where(iota((heads, HD), 1) < HD // 2, top, total)
    for q in range(heads // NS):
        soft_s[pl.ds(q, NS, stride=8), :] = acc[q * NS : (q + 1) * NS, :]
        soft_s[pl.ds(q + 4, NS, stride=8), :] = state[q * NS : (q + 1) * NS, :]
    soft_r[rows(me * 8, 8), :] = soft_s[rows(me * 8, 8), :]

    def soft(i, way):
        other = lax.rem(me + i, NS)
        return remote(
            soft_s.at[rows(other * 8, 8)],
            soft_r.at[rows(way * 8, 8)],
            seq_ss.at[1, other],
            seq_rs.at[1, way],
            seq=other,
        )

    def soft_start(i, carry):
        soft(i, me).start()
        return carry

    def soft_wait(i, carry):
        soft(i, lax.rem(me + i, NS)).wait_recv()
        return carry

    lax.fori_loop(1, NS, soft_start, 0)

    for j in range(NT):
        load_o(0, j).wait()
        own_v[0, j] = project(0, 0, j)
        own_v[1, j] = project(1, 0, j)

    lax.fori_loop(1, NS, soft_wait, 0)
    joined = []
    for q in range(heads // NS):
        sums = soft_r[pl.ds(q, NS, stride=8), :]
        both = soft_r[pl.ds(q + 4, NS, stride=8), :]
        tops = both[:, 0:1]
        weight = jnp.exp2((tops - jnp.max(tops, axis=0, keepdims=True)) * (SCALE * LOG2E))
        whole = jnp.sum(weight * both[:, HD // 2 : HD // 2 + 1], axis=0, keepdims=True)
        joined.append(jnp.sum(weight * sums, axis=0, keepdims=True) / whole)
    for q in range(heads // NS):
        join_s[q : q + 1, :] = joined[q]
        join_s[q + 4 : q + 5, :] = joined[q]
    join_r[rows(me * 8, 8), :] = join_s[...]

    def join(i, way):
        other = lax.rem(me + i, NS)
        return remote(
            join_s, join_r.at[rows(way * 8, 8)], seq_ss.at[2, other], seq_rs.at[2, way], seq=other
        )

    def join_start(i, carry):
        join(i, me).start()
        return carry

    def join_wait(i, carry):
        join(i, lax.rem(me + i, NS)).wait_recv()
        return carry

    lax.fori_loop(1, NS, join_start, 0)

    for j in range(NT):
        send(0, 1, 2, j, far=0, loaded=True)

    lax.fori_loop(1, NS, join_wait, 0)
    for head in range(GROUP):
        start = (head % 2) * ROWS * 8 + head // 2
        da_v[:, head * HD : (head + 1) * HD] = join_r[pl.ds(start, ROWS, stride=8), :].astype(BF16)

    def dpart(k):
        return remote(
            dpart_s.at[k],
            dpart_r.at[k],
            dpart_ss.at[k],
            dpart_rs.at[k],
            head=lax.rem(y + k, NH),
        )

    def dec_project(k):
        return jnp.concatenate([dot(da_v[...], wo_v[k, j]) for j in range(NT)], axis=1)

    for k in (2, 1, 3):
        dpart_s[k] = dec_project(k).astype(BF16)
        dpart(k).start()
    dec_own = dec_project(0)

    for j in range(NT):
        send(1, 3, 5, j, far=1, loaded=True)

    for k in (1, 3, 2):
        dpart(k).wait_recv()
        dec_own = dec_own + dpart_r[k].astype(F32)
    for t in range(STEPS):
        dout_v[t] = dec_own[t * SLOTS : (t + 1) * SLOTS].astype(BF16)

    for j in range(NT):
        for half in range(2):
            part(2 + half, j).wait_recv()
            part(4 + half, j).wait_recv()
            value = own_v[half, j] + part_r[2 + half, j].astype(F32)
            value = (value + part_r[4 + half, j].astype(F32)).astype(BF16)
            for p in range(2):
                to = p * LP + half * HALF
                out_v[to : to + HALF, j * TILE : (j + 1) * TILE] = value[p * HALF : (p + 1) * HALF]

    def settle(i, carry):
        hand(i, me).wait_send()
        soft(i, me).wait_send()
        join(i, me).wait_send()
        return carry

    lax.fori_loop(1, NS, settle, 0)
    for k in range(1, NH):
        dpart(k).wait_send()
    for slot in range(6):
        for j in range(NT):
            part(slot, j).wait_send()


def save(out_v, hand_v, dout_v, out, handed, dec_out, sem):
    copies = [
        pltpu.make_async_copy(out_v, out, sem.at[0]),
        pltpu.make_async_copy(hand_v, handed, sem.at[1]),
        pltpu.make_async_copy(dout_v, dec_out, sem.at[2]),
    ]
    for copy in copies:
        copy.start()
    for copy in copies:
        copy.wait()


def local(
    prompts,
    prompt_len,
    admitted,
    cache_len,
    cache_kv,
    dec_tokens,
    w_query,
    w_key,
    w_value,
    w_out,
    q_gain,
    k_gain,
):
    half = HD // 2
    one = (THETA ** (-np.arange(half, dtype=np.float64) / half)).astype(np.float32)
    freq = jnp.asarray(np.concatenate([one, one])[None, :])
    smem = pl.BlockSpec(memory_space=pltpu.SMEM)
    vmem = pl.BlockSpec(memory_space=pltpu.VMEM)
    hbm = pl.BlockSpec(memory_space=pl.ANY)
    dma = pltpu.SemaphoreType.DMA
    shapes = [(2 * LP, WIDTH), (2 * LP, 2 * HD), (STEPS, SLOTS, WIDTH)]
    results = pl.pallas_call(
        kernel,
        out_shape=[pltpu.VMEM(shape, BF16) for shape in shapes],
        in_specs=[smem] * 3 + [vmem] * 3 + [hbm] * 7,
        out_specs=[vmem] * 3,
        scratch_shapes=[
            pltpu.VMEM((2 * LP + ROWS, D), BF16),
            pltpu.VMEM((STEPS, SLOTS, D), BF16),
            pltpu.VMEM((D, 2 * HD), BF16),
            pltpu.VMEM((NT, D, TILE), BF16),
            pltpu.VMEM((NH, NT, WIDTH, TILE), BF16),
            pltpu.VMEM((SLOTS * CACHE, 2 * HD), BF16),
            pltpu.VMEM((2, 4, HALF, HD), F32),
            pltpu.VMEM((2 * LP, 2 * HD), BF16),
            pltpu.VMEM((2 * LP, 2 * HD), BF16),
            pltpu.VMEM((2, GROUP * HALF, HD), BF16),
            pltpu.VMEM((GROUP * ROWS, HD), BF16),
            pltpu.VMEM((HD, 2 * HD), BF16),
            pltpu.VMEM((2, LP, WIDTH), BF16),
            pltpu.VMEM((6, NT, LP, TILE), BF16),
            pltpu.VMEM((6, NT, LP, TILE), BF16),
            pltpu.VMEM((2, NT, LP, TILE), F32),
            pltpu.VMEM((NS * 8, HD), F32),
            pltpu.VMEM((NS * 8, HD), F32),
            pltpu.VMEM((8, HD), F32),
            pltpu.VMEM((NS * 8, HD), F32),
            pltpu.VMEM((ROWS, WIDTH), BF16),
            pltpu.VMEM((NH, ROWS, WIDTH), BF16),
            pltpu.VMEM((NH, ROWS, WIDTH), BF16),
            dma((2, 2)),
            dma((4,)),
            dma((NT,)),
            dma((NH, NT)),
            dma((6, NT)),
            dma((6, NT)),
            dma((3, NS)),
            dma((3, NS)),
            dma((NH,)),
            dma((NH,)),
        ],
        compiler_params=pltpu.CompilerParams(
            collective_id=0, has_side_effects=True, vmem_limit_bytes=52 * 2**20
        ),
        cost_estimate=pl.CostEstimate(
            flops=10_500_000_000, bytes_accessed=25_000_000, transcendentals=2_000_000
        ),
    )(
        prompt_len,
        admitted,
        cache_len,
        freq,
        q_gain[None, :],
        k_gain[None, :],
        prompts.reshape(2 * LP, D),
        dec_tokens,
        w_query,
        w_key,
        w_value,
        w_out,
        cache_kv.reshape(SLOTS * CACHE, 2 * HD),
    )
    out, handed, decoded = pl.pallas_call(
        save,
        out_shape=[jax.ShapeDtypeStruct(shape, BF16) for shape in shapes],
        in_specs=[vmem] * 3,
        out_specs=[hbm] * 3,
        scratch_shapes=[dma((3,))],
    )(*results)
    return (
        out.reshape(2, LP, WIDTH),
        handed.reshape(1, 2 * NS, EACH, 2 * HD),
        decoded,
    )


def solution(mesh):
    placed = (
        P("seq", None, None),
        P(),
        P(),
        P(),
        P("head", None, "seq", None),
        P(),
        P(None, "head"),
        P(None, "head"),
        P(None, "head"),
        P("head", None),
        P(),
        P(),
    )
    return jax.shard_map(
        local,
        mesh=mesh,
        in_specs=placed,
        out_specs=(P("seq", None, "head"), P("head", None, "seq", None), P(None, None, "head")),
        check_vma=False,
    )
```

time: 76.7 us -> 73.9 us (0.963)
  Pallas kernels: 68.9 us -> 65.7 us
    pallas_call x1 -> x2, Pallas kernels: 68.9 us -> 65.7 us  [the longest x1 63.3 us: local(): pl.pallas_call(kernel, out_shape=[pltpu.VMEM(shape, BF16) for shape in sh...]
    unnamed x2 -> x20, local copies, waits for them, and re-layouts: 3.93 us -> 7.09 us
    reshape x2 -> x0, local copies, waits for them, and re-layouts: 2.99 us -> none  [the longest x1 1.59 us: local(): dec_tokens.reshape(ROWS, D)]
where the time goes in v1:
time: 73.9 us; the launch traced here: 73.7 us
  Pallas kernels  65.7 us (89%)
  local copies, waits for them, and re-layouts  7.09 us (10%)
  between operations  0.83 us (1%)
    pallas_call x1, Pallas kernels, local(): pl.pallas_call(kernel, out_shape=[pltpu.VMEM(shape, BF16) for shape in sh...  63.3 us
    unnamed x20, local copies, waits for them, and re-layouts  7.09 us
    pallas_call x1, Pallas kernels, local(): pl.pallas_call(save, out_shape=[jax.ShapeDtypeStruct(shape, BF16) for sha...  2.39 us

profile of v1, /device:TPU:1, one launch (start us, length us, event | category | flops | bytes accessed | tf_op | source)
XLA Modules:
  0.0 73.7 jit_solution(3739331484352109069)
XLA Ops:
  0.6 0.0 copy-start.3
  0.6 0.9 %copy-done.3 = bf16[4,4,4096]{2,1,0:T(4,128)(2,1)S(1)} copy-done((bf16[4,4,4096]{2,1,0:T(4,128)(2,1)S(1)}, bf16[4,4,4096]{2,1,0:T(4,128)(2,1)}, u32[]{:S(2)}) %copy-start.3) | copy-done | bytes 131096
  1.5 0.0 copy-start.4
  1.5 0.7 copy-done.4
  2.2 0.0 copy-start.5
  2.2 0.7 copy-done.5
  2.9 0.0 copy-start.6
  2.9 0.7 copy-done.6
  3.5 0.0 copy-start.7
  3.5 0.7 copy-done.7
  4.2 0.0 copy-start.8
  4.2 0.7 copy-done.8
  4.8 0.0 copy-start.9
  4.8 0.7 copy-done.9
  5.5 63.3 %shard_map.148 = (bf16[512,1024]{1,0:T(8,128)(2,1)S(1)}, bf16[512,256]{1,0:T(8,128)(2,1)S(1)}, bf16[4,4,1024]{2,1,0:T(4,128)(2,1)S(1)}) custom-call(s32[64]{0:T(128)S(1)} %copy-done.4, s32[4]{0:T(128)S(1)} %copy-done.5, s32[4]{0:T(128)S(1)} %copy-done.6, f32[1,128]{1,0:T(1,128)S(1)} %copy-done.9, f32[1,128]{1,0:T(1,128)S(1)} %bitcast.6, ...), custom_call_target="tpu_custom_call" | custom-call | flops 10499999744 | bytes 25000000 | tf_op jit(solution)/shard_map/pallas_call | solution.py:527
  68.8 0.0 copy-start
  68.8 1.0 %copy-done = bf16[512,1024]{1,0:T(8,128)(2,1)} copy-done((bf16[512,1024]{1,0:T(8,128)(2,1)}, bf16[512,1024]{1,0:T(8,128)(2,1)S(1)}, u32[]{:S(2)}) %copy-start) | copy-done | bytes 1048600
  69.8 0.0 copy-start.1
  69.8 0.7 copy-done.1
  70.5 0.0 copy-start.2
  70.5 0.6 copy-done.2
  71.1 2.4 %shard_map.149 = (bf16[512,1024]{1,0:T(8,128)(2,1)}, bf16[512,256]{1,0:T(8,128)(2,1)}, bf16[4,4,1024]{2,1,0:T(4,128)(2,1)}) custom-call(bf16[512,1024]{1,0:T(8,128)(2,1)} %copy-done, bf16[512,256]{1,0:T(8,128)(2,1)} %copy-done.1, bf16[4,4,1024]{2,1,0:T(4,128)(2,1)} %copy-done.2), custom_call_target="tpu_custom_call" | custom-call | tf_op jit(solution)/shard_map/pallas_call | solution.py:588
Async XLA Ops:
  0.6 0.9 %copy-start.3 = (bf16[4,4,4096]{2,1,0:T(4,128)(2,1)S(1)}, bf16[4,4,4096]{2,1,0:T(4,128)(2,1)}, u32[]{:S(2)}) copy-start(bf16[4,4,4096]{2,1,0:T(4,128)(2,1)} %dec.1) | copy-start | bytes 393220
  1.5 0.7 copy-start.4
  2.2 0.7 copy-start.5
  2.9 0.7 copy-start.6
  3.5 0.7 copy-start.7
  4.2 0.7 copy-start.8
  4.8 0.7 copy-start.9
  68.8 1.0 %copy-start = (bf16[512,1024]{1,0:T(8,128)(2,1)}, bf16[512,1024]{1,0:T(8,128)(2,1)S(1)}, u32[]{:S(2)}) copy-start(bf16[512,1024]{1,0:T(8,128)(2,1)S(1)} %get-tuple-element.9.out_v) | copy-start | bytes 3145732
  69.8 0.7 copy-start.1
  70.5 0.6 copy-start.2

commit v2 on v1

v2 whole, which is shorter than its diff:
```python
import functools

import jax
import jax.numpy as jnp
import numpy as np
from jax import lax
from jax.experimental import pallas as pl
from jax.experimental.pallas import tpu as pltpu
from jax.sharding import PartitionSpec as P

D = 4096
HD = 128
GROUP = 8
WIDTH = GROUP * HD
LP = 256
HALF = LP // 2
SLOTS = 4
STEPS = 4
ROWS = SLOTS * STEPS
CACHE = 512
NS = 32
NH = 4
EACH = LP // NS
EPS = 1e-06
THETA = 1000000.0
NEG = -1e30
SCALE = HD ** (-0.5)
LOG2E = 1.4426950408889634
TILE = 256
NT = WIDTH // TILE
F32 = jnp.float32
BF16 = jnp.bfloat16


def dot(a, b):
    return jnp.dot(a, b, preferred_element_type=F32)


def dot_nt(a, b):
    return lax.dot_general(a, b, (((1,), (1,)), ((), ())), preferred_element_type=F32)


def iota(shape, dim):
    return lax.broadcasted_iota(jnp.int32, shape, dim)


def rotation(positions, freq):
    angle = positions.astype(F32) * freq
    sign = jnp.where(iota((1, HD), 1) < HD // 2, -1.0, 1.0)
    return jnp.cos(angle), jnp.sin(angle) * sign


def gained(cosine, sine, gain):
    return cosine * gain, sine * pltpu.roll(gain, HD // 2, 1)


def normrot(a, first, second):
    inverse = lax.rsqrt(jnp.mean(a * a, axis=-1, keepdims=True) + EPS)
    return (a * first + pltpu.roll(a, HD // 2, 1) * second) * inverse


def kernel(
    plen_ref,
    adm_ref,
    clen_ref,
    freq_ref,
    qg_ref,
    kg_ref,
    prompts,
    dec,
    wq,
    wk,
    wv,
    wo,
    cache,
    out,
    handed,
    dec_out,
    plen,
    adm,
    clen,
    row_v,
    x_v,
    dec_v,
    w_v,
    wo_v,
    cache_v,
    tab_v,
    f_v,
    kv_v,
    give_v,
    hand_v,
    q_v,
    dq_v,
    dkv_v,
    pa_v,
    part_s,
    part_r,
    own_v,
    soft_s,
    soft_r,
    join_s,
    join_r,
    da_v,
    dpart_s,
    dpart_r,
    out_v,
    dout_v,
    small_sem,
    x_sem,
    in_sem,
    w_sem,
    wo_sem,
    out_sem,
    part_ss,
    part_rs,
    seq_ss,
    seq_rs,
    dpart_ss,
    dpart_rs,
):
    y = lax.axis_index("head")
    me = lax.axis_index("seq")
    right = lax.rem(y + 1, NH)
    left = lax.rem(y + NH - 1, NH)

    def remote(src, dst, send, recv, **where):
        return pltpu.make_async_remote_copy(
            src_ref=src,
            dst_ref=dst,
            send_sem=send,
            recv_sem=recv,
            device_id=where,
            device_id_type=pl.DeviceIdType.MESH,
        )

    def landed(ref, sem):
        pltpu.make_async_copy(ref, ref, sem).wait()

    def rows(start, size):
        return pl.ds(pl.multiple_of(start, size), size)

    def load_x(half, p):
        source = p * LP + half * HALF
        target = half * (LP + ROWS) + p * HALF
        return pltpu.make_async_copy(
            prompts.at[source : source + HALF], x_v.at[target : target + HALF], x_sem.at[half]
        )

    small = [
        pltpu.make_async_copy(ref, to, small_sem.at[i])
        for ref, to, i in (
            (freq_ref, row_v.at[0], 0),
            (qg_ref, row_v.at[1], 0),
            (kg_ref, row_v.at[2], 0),
            (plen_ref, plen, 1),
            (adm_ref, adm, 2),
            (clen_ref, clen, 3),
        )
    ]
    load_k = pltpu.make_async_copy(wk, w_v.at[0, :, 0:HD], w_sem.at[0])
    load_v = pltpu.make_async_copy(wv, w_v.at[0, :, HD : 2 * HD], w_sem.at[0])
    load_dec = pltpu.make_async_copy(dec, dec_v, in_sem.at[0])
    load_cache = pltpu.make_async_copy(cache, cache_v, in_sem.at[1])

    def load_q(t):
        return pltpu.make_async_copy(wq.at[:, rows((t - 1) * TILE, TILE)], w_v.at[t], w_sem.at[t])

    def load_o(k, j):
        start = lax.rem(y + k, NH) * WIDTH + j * TILE
        sem = wo_sem.at[j if k in (2, 3) else NT + k]
        return pltpu.make_async_copy(wo.at[:, rows(start, TILE)], wo_v.at[k, j], sem)

    load_dec.start()
    load_k.start()
    load_v.start()
    load_x(0, 0).start()
    load_x(0, 1).start()
    for load in small:
        load.start()

    barrier = pltpu.get_barrier_semaphore()

    def greet(i, carry):
        pl.semaphore_signal(
            barrier,
            inc=1,
            device_id={"seq": lax.rem(me + i, NS)},
            device_id_type=pl.DeviceIdType.MESH,
        )
        return carry

    for k in range(1, NH):
        pl.semaphore_signal(
            barrier,
            inc=1,
            device_id={"head": lax.rem(y + k, NH)},
            device_id_type=pl.DeviceIdType.MESH,
        )
    lax.fori_loop(1, NS, greet, 0)

    load_q(1).start()
    load_q(2).start()

    landed(row_v, small_sem.at[0])
    for load in small[3:]:
        load.wait()
    freq, q_gain, k_gain = row_v[0], row_v[1], row_v[2]
    for half in range(2):
        first, second = rotation(iota((HALF, HD), 0) + half * HALF, freq)
        tab_v[half, 0], tab_v[half, 1] = gained(first, second, q_gain)
        tab_v[half, 2], tab_v[half, 3] = gained(first, second, k_gain)
    admitted = [adm[r] for r in range(SLOTS)]
    handed_len = [plen[jnp.maximum(admitted[r], 0)] for r in range(SLOTS)]
    is_new = [admitted[r] >= 0 for r in range(SLOTS)]
    eff_len = [jnp.where(is_new[r], handed_len[r], clen[r]) for r in range(SLOTS)]

    def per_slot(slot, values):
        picked = jnp.full(slot.shape, values[0], jnp.int32)
        for r in range(1, SLOTS):
            picked = jnp.where(slot == r, values[r], picked)
        return picked

    token = iota((ROWS, HD), 0)
    places = per_slot(token & (SLOTS - 1), eff_len) + (token >> 2)
    first, second = rotation(places, freq)
    dq_first, dq_second = gained(first, second, q_gain)
    dk_first, dk_second = gained(first, second, k_gain)

    load_dec.wait()
    x_v[LP : LP + ROWS, :] = jnp.concatenate(
        [dec_v[t].astype(F32) for t in range(STEPS)], axis=0
    ).astype(BF16)

    def finish_query(half, t, count):
        slot = lax.rem(t + 5, 6)
        for b in range(TILE // HD):
            mine = f_v[t, 0:count, b * HD : (b + 1) * HD]
            for p in range(2):
                one = normrot(mine[p * HALF : (p + 1) * HALF], tab_v[half, 0], tab_v[half, 1])
                q_v[p, rows(slot * TILE + b * HD, HD), :] = one.astype(BF16)
            if half == 0:
                one = normrot(mine[LP : LP + ROWS], dq_first, dq_second)
                dq_v[rows((slot * 2 + b) * ROWS, ROWS), :] = one.astype(BF16)

    def multiply(half, after_keys=None):
        start = half * (LP + ROWS)
        count = LP if half else LP + ROWS

        def tile(t, carry):
            if half == 0:
                landed(w_v.at[t], w_sem.at[t])

                @pl.when(t < NT - 2)
                def _():
                    load_q(t + 3).start()

                @pl.when(t < NT)
                def _():
                    load_o(2, t).start()
                    load_o(3, t).start()

            if after_keys is not None:
                pl.when(t == 1)(after_keys)

            finish_query(half, lax.rem(t + 5, 6), count)
            f_v[t, 0:count, :] = dot(x_v[start : start + count, :], w_v[t])
            return carry

        lax.fori_loop(0, 1 + NT, tile, 0)
        finish_query(half, NT, count)

    def keys_values(half):
        for p in range(2):
            mine = f_v[0, p * HALF : (p + 1) * HALF, :]
            to = slice(p * LP + half * HALF, p * LP + (half + 1) * HALF)
            key = normrot(mine[:, 0:HD], tab_v[half, 2], tab_v[half, 3])
            kv_v[to, 0:HD] = key.astype(BF16)
            kv_v[to, HD : 2 * HD] = mine[:, HD : 2 * HD].astype(BF16)
        if half == 0:
            new = f_v[0, LP : LP + ROWS, :]
            dkv_v[...] = jnp.zeros_like(dkv_v)
            dkv_v[0:ROWS, 0:HD] = normrot(new[:, 0:HD], dk_first, dk_second).astype(BF16)
            dkv_v[0:ROWS, HD : 2 * HD] = new[:, HD : 2 * HD].astype(BF16)

    def attend(half):
        keys = (half + 1) * HALF
        at = iota((keys, HALF), 0)
        causal = at <= iota((keys, HALF), 1) + half * HALF
        for p in range(2):
            bias = jnp.where(causal & (at < plen[2 * me + p]), 0.0, NEG)
            scores = dot_nt(kv_v[p * LP : p * LP + keys, 0:HD], q_v[p, 0 : GROUP * HALF])
            scores = scores + jnp.concatenate([bias] * GROUP, axis=1)
            top = jnp.max(scores, axis=0, keepdims=True)
            expo = jnp.exp2((scores - top) * (SCALE * LOG2E))
            weights = expo * (1.0 / jnp.sum(expo, axis=0, keepdims=True))
            values = kv_v[p * LP : p * LP + keys, HD : 2 * HD].astype(F32).T.astype(BF16)
            mixed = dot(values, weights.astype(BF16))
            for head in range(GROUP):
                one = mixed[:, head * HALF : (head + 1) * HALF].T.astype(BF16)
                pa_v[half, p * HALF : (p + 1) * HALF, head * HD : (head + 1) * HD] = one

    def part(slot, j):
        to = right if slot in (0, 2, 3) else left
        return remote(
            part_s.at[slot, j],
            part_r.at[slot, j],
            part_ss.at[0],
            part_rs.at[slot, 0 if slot in (3, 4) else j],
            head=to,
        )

    def send_all(half, targets, tiles, far=None, load=False):
        def tile(j, carry):
            if load:
                landed(wo_v.at[2:4, j], wo_sem.at[j])
            if far is not None:
                landed(part_r.at[far, j], part_rs.at[far, j])
            values = [dot(pa_v[half], wo_v[k, j]) for k, slot in targets]
            for (k, slot), value in zip(targets, values):
                if far is not None:
                    value = value + part_r[far, j].astype(F32)
                part_s[slot, j] = value.astype(BF16)
                part(slot, j).start()
            return carry

        lax.fori_loop(*tiles, tile, 0)

    landed(x_v.at[0:LP], x_sem.at[0])
    multiply(0)
    load_x(1, 0).start()
    load_x(1, 1).start()
    for j in range(NT):
        load_o(1, j).start()
    for j in range(NT):
        load_o(0, j).start()
    load_cache.start()
    keys_values(0)
    attend(0)
    pl.semaphore_wait(barrier, NS - 1 + NH - 1)
    send_all(0, ((2, 0), (3, 4)), (0, NT), load=True)

    landed(x_v.at[LP + ROWS : 2 * LP + ROWS], x_sem.at[1])
    def hand(i, way):
        other = lax.rem(me + i, NS)
        return remote(
            give_v.at[rows(other * 16, 16)],
            hand_v.at[rows(way * 16, 16)],
            seq_ss.at[0],
            seq_rs.at[0],
            seq=other,
        )

    def hand_over():
        keys_values(1)
        place = iota((2 * LP, 2 * LP), 0)
        source = (((place >> 3) & 1) << 8) + ((place & 7) << 5) + (place >> 4)
        pick = jnp.where(source == iota((2 * LP, 2 * LP), 1), 1.0, 0.0).astype(BF16)
        give_v[...] = dot(pick, kv_v[...]).astype(BF16)
        hand_v[rows(me * 16, 16), :] = give_v[rows(me * 16, 16), :]

        def hand_start(i, carry):
            hand(i, me).start()
            return carry

        lax.fori_loop(1, NS, hand_start, 0)

    multiply(1, hand_over)
    attend(1)
    landed(wo_v.at[1], wo_sem.at[NT + 1])
    send_all(1, ((1, 3), (2, 1)), (0, NT))
    load_cache.wait()

    landed(hand_v.at[0 : (NS - 1) * 16], seq_rs.at[0])
    save_hand = pltpu.make_async_copy(hand_v, handed, out_sem.at[0])
    save_hand.start()

    heads = GROUP * ROWS
    queries = dq_v[0:heads]

    def pieces():
        for r in range(SLOTS):
            slot = iota((heads, CACHE), 0) & (SLOTS - 1)
            at = (iota((heads, CACHE), 1) << 5) + me
            limit = jnp.where(is_new[r], 0, clen[r])
            yield (
                dot_nt(queries, cache_v[r * CACHE : (r + 1) * CACHE, 0:HD]),
                (slot == r) & (at < limit),
                cache_v[r * CACHE : (r + 1) * CACHE, HD : 2 * HD],
            )
        slot = iota((heads, 2 * LP), 0) & (SLOTS - 1)
        column = iota((heads, 2 * LP), 1)
        prompt = column >> 3
        at = ((column & 7) << 5) + me
        yield (
            dot_nt(queries, hand_v[:, 0:HD]),
            (prompt == per_slot(slot, admitted)) & (at < per_slot(slot, handed_len)),
            hand_v[:, HD : 2 * HD],
        )
        row = iota((heads, HD), 0)
        column = iota((heads, HD), 1) + jnp.where(me == 0, 0, ROWS)
        yield (
            dot_nt(queries, dkv_v[:, 0:HD]),
            ((row & 3) == (column & 3)) & ((column >> 2) <= ((row >> 2) & 3)) & (column < ROWS),
            dkv_v[:, HD : 2 * HD],
        )

    parts = [(jnp.where(mask, s, NEG), mask, v) for s, mask, v in pieces()]
    top = functools.reduce(jnp.maximum, [jnp.max(s, axis=-1, keepdims=True) for s, _, _ in parts])
    total = jnp.zeros((heads, 1), F32)
    acc = jnp.zeros((heads, HD), F32)
    for s, mask, v in parts:
        expo = jnp.where(mask, jnp.exp2((s - top) * (SCALE * LOG2E)), 0.0)
        total = total + jnp.sum(expo, axis=-1, keepdims=True)
        acc = acc + dot(expo.astype(BF16), v)
    state = jnp.where(iota((heads, HD), 1) < HD // 2, top, total)
    for q in range(heads // NS):
        soft_s[pl.ds(q, NS, stride=8), :] = acc[q * NS : (q + 1) * NS, :]
        soft_s[pl.ds(q + 4, NS, stride=8), :] = state[q * NS : (q + 1) * NS, :]
    soft_r[rows(me * 8, 8), :] = soft_s[rows(me * 8, 8), :]

    def soft(i, way):
        other = lax.rem(me + i, NS)
        return remote(
            soft_s.at[rows(other * 8, 8)],
            soft_r.at[rows(way * 8, 8)],
            seq_ss.at[1],
            seq_rs.at[1],
            seq=other,
        )

    def soft_start(i, carry):
        soft(i, me).start()
        return carry

    lax.fori_loop(1, NS, soft_start, 0)

    send_all(0, ((1, 2),), (0, NT), far=0)

    landed(wo_v.at[0], wo_sem.at[NT])

    def own(j, carry):
        own_v[0, j] = dot(pa_v[0], wo_v[0, j])
        own_v[1, j] = dot(pa_v[1], wo_v[0, j])
        return carry

    lax.fori_loop(0, NT, own, 0)

    landed(soft_r.at[0 : (NS - 1) * 8], seq_rs.at[1])
    joined = []
    for q in range(heads // NS):
        sums = soft_r[pl.ds(q, NS, stride=8), :]
        both = soft_r[pl.ds(q + 4, NS, stride=8), :]
        tops = both[:, 0:1]
        weight = jnp.exp2((tops - jnp.max(tops, axis=0, keepdims=True)) * (SCALE * LOG2E))
        whole = jnp.sum(weight * both[:, HD // 2 : HD // 2 + 1], axis=0, keepdims=True)
        joined.append(jnp.sum(weight * sums, axis=0, keepdims=True) / whole)
    for q in range(heads // NS):
        join_s[q : q + 1, :] = joined[q]
        join_s[q + 4 : q + 5, :] = joined[q]
    join_r[rows(me * 8, 8), :] = join_s[...]

    def join(i, way):
        other = lax.rem(me + i, NS)
        return remote(
            join_s, join_r.at[rows(way * 8, 8)], seq_ss.at[2], seq_rs.at[2], seq=other
        )

    def join_start(i, carry):
        join(i, me).start()
        return carry

    lax.fori_loop(1, NS, join_start, 0)


    send_all(1, ((3, 5),), (0, NT - 1), far=1)
    landed(join_r.at[0 : (NS - 1) * 8], seq_rs.at[2])
    for head in range(GROUP):
        start = (head % 2) * ROWS * 8 + head // 2
        da_v[:, head * HD : (head + 1) * HD] = join_r[pl.ds(start, ROWS, stride=8), :].astype(BF16)

    def dpart(k):
        return remote(
            dpart_s.at[k],
            dpart_r.at[k],
            dpart_ss.at[0],
            dpart_rs.at[0],
            head=lax.rem(y + k, NH),
        )

    def dec_project(k):
        return jnp.concatenate([dot(da_v[...], wo_v[k, j]) for j in range(NT)], axis=1)

    for k in (2, 1, 3):
        dpart_s[k] = dec_project(k).astype(BF16)
        dpart(k).start()
    dec_own = dec_project(0)

    send_all(1, ((3, 5),), (NT - 1, NT), far=1)
    landed(hand_v.at[0 : (NS - 1) * 16], seq_ss.at[0])
    landed(soft_r.at[0 : (NS - 1) * 8], seq_ss.at[1])
    landed(join_r.at[0 : (NS - 1) * 8], seq_ss.at[2])
    save_hand.wait()

    landed(part_r.at[3], part_rs.at[3, 0])
    landed(part_r.at[4], part_rs.at[4, 0])

    def finish(j, carry):
        for half in range(2):
            late = 5 if half else 2
            landed(part_r.at[late, j], part_rs.at[late, j])
        for half in range(2):
            value = own_v[half, j] + part_r[2 + half, j].astype(F32)
            value = (value + part_r[4 + half, j].astype(F32)).astype(BF16)
            for p in range(2):
                out_v[half, j, p] = value[p * HALF : (p + 1) * HALF]
            pltpu.make_async_copy(
                out_v.at[half, j],
                out.at[:, half * HALF : (half + 1) * HALF, rows(j * TILE, TILE)],
                out_sem.at[2],
            ).start()
        return carry

    lax.fori_loop(0, NT, finish, 0)

    landed(dpart_r.at[1:NH], dpart_rs.at[0])
    for k in (1, 3, 2):
        dec_own = dec_own + dpart_r[k].astype(F32)
    for t in range(STEPS):
        dout_v[t] = dec_own[t * SLOTS : (t + 1) * SLOTS].astype(BF16)
    save_dec = pltpu.make_async_copy(dout_v, dec_out, out_sem.at[1])
    save_dec.start()

    landed(dpart_s.at[1:NH], dpart_ss.at[0])
    landed(part_s, part_ss.at[0])
    landed(out_v, out_sem.at[2])
    save_dec.wait()


def local(
    prompts,
    prompt_len,
    admitted,
    cache_len,
    cache_kv,
    dec_tokens,
    w_query,
    w_key,
    w_value,
    w_out,
    q_gain,
    k_gain,
):
    half = HD // 2
    one = (THETA ** (-np.arange(half, dtype=np.float64) / half)).astype(np.float32)
    freq = jnp.asarray(np.concatenate([one, one])[None, :])
    hbm = pl.BlockSpec(memory_space=pl.ANY)
    dma = pltpu.SemaphoreType.DMA
    shapes = [(2, LP, WIDTH), (2 * LP, 2 * HD), (STEPS, SLOTS, WIDTH)]
    out, handed, decoded = pl.pallas_call(
        kernel,
        out_shape=[pltpu.VMEM(shape, BF16) for shape in shapes],
        in_specs=[hbm] * 13,
        out_specs=[hbm] * 3,
        scratch_shapes=[
            pltpu.SMEM((2 * NS,), jnp.int32),
            pltpu.SMEM((SLOTS,), jnp.int32),
            pltpu.SMEM((SLOTS,), jnp.int32),
            pltpu.VMEM((3, 1, HD), F32),
            pltpu.VMEM((2 * LP + ROWS, D), BF16),
            pltpu.VMEM((STEPS, SLOTS, D), BF16),
            pltpu.VMEM((1 + NT, D, TILE), BF16),
            pltpu.VMEM((NH, NT, WIDTH, TILE), BF16),
            pltpu.VMEM((SLOTS * CACHE, 2 * HD), BF16),
            pltpu.VMEM((2, 4, HALF, HD), F32),
            pltpu.VMEM((2 + NT, LP + ROWS, TILE), F32),
            pltpu.VMEM((2 * LP, 2 * HD), BF16),
            pltpu.VMEM((2 * LP, 2 * HD), BF16),
            pltpu.VMEM((2 * LP, 2 * HD), BF16),
            pltpu.VMEM((2, (GROUP + 4) * HALF, HD), BF16),
            pltpu.VMEM(((GROUP + 4) * ROWS, HD), BF16),
            pltpu.VMEM((HD, 2 * HD), BF16),
            pltpu.VMEM((2, LP, WIDTH), BF16),
            pltpu.VMEM((6, NT, LP, TILE), BF16),
            pltpu.VMEM((6, NT, LP, TILE), BF16),
            pltpu.VMEM((2, NT, LP, TILE), F32),
            pltpu.VMEM((NS * 8, HD), F32),
            pltpu.VMEM((NS * 8, HD), F32),
            pltpu.VMEM((8, HD), F32),
            pltpu.VMEM((NS * 8, HD), F32),
            pltpu.VMEM((ROWS, WIDTH), BF16),
            pltpu.VMEM((NH, ROWS, WIDTH), BF16),
            pltpu.VMEM((NH, ROWS, WIDTH), BF16),
            pltpu.VMEM((2, NT, 2, HALF, TILE), BF16),
            pltpu.VMEM((STEPS, SLOTS, WIDTH), BF16),
            dma((4,)),
            dma((2,)),
            dma((2,)),
            dma((1 + NT,)),
            dma((NT + 2,)),
            dma((3,)),
            dma((1,)),
            dma((6, NT)),
            dma((3,)),
            dma((3,)),
            dma((1,)),
            dma((1,)),
        ],
        compiler_params=pltpu.CompilerParams(
            collective_id=0, has_side_effects=True, vmem_limit_bytes=56 * 2**20
        ),
        cost_estimate=pl.CostEstimate(
            flops=10_500_000_000, bytes_accessed=25_000_000, transcendentals=2_000_000
        ),
    )(
        prompt_len,
        admitted,
        cache_len,
        freq,
        q_gain[None, :],
        k_gain[None, :],
        prompts.reshape(2 * LP, D),
        dec_tokens,
        w_query,
        w_key,
        w_value,
        w_out,
        cache_kv.reshape(SLOTS * CACHE, 2 * HD),
    )
    return (
        out,
        handed.reshape(1, 2 * NS, EACH, 2 * HD),
        decoded,
    )


def solution(mesh):
    placed = (
        P("seq", None, None),
        P(),
        P(),
        P(),
        P("head", None, "seq", None),
        P(),
        P(None, "head"),
        P(None, "head"),
        P(None, "head"),
        P("head", None),
        P(),
        P(),
    )
    return jax.shard_map(
        local,
        mesh=mesh,
        in_specs=placed,
        out_specs=(P("seq", None, "head"), P("head", None, "seq", None), P(None, None, "head")),
        check_vma=False,
    )
```

time: 73.9 us -> 50.3 us (0.68)
  Pallas kernels: 65.7 us -> 47.1 us
  local copies, waits for them, and re-layouts: 7.09 us -> 2.29 us
    pallas_call x1, Pallas kernels: 63.3 us -> 47.1 us  [local(): pl.pallas_call(kernel, out_shape=[pltpu.VMEM(shape, BF16) for shape in sh...]
    unnamed x20 -> x3, local copies, waits for them, and re-layouts: 7.09 us -> 2.29 us
    pallas_call x1 -> x0, Pallas kernels: 2.39 us -> none  [local(): pl.pallas_call(save, out_shape=[jax.ShapeDtypeStruct(shape, BF16) for sha...]
where the time goes in v2:
time: 50.3 us; the launch traced here: 50 us
  Pallas kernels  47.1 us (94%)
  local copies, waits for them, and re-layouts  2.29 us (5%)
  between operations  0.64 us (1%)
    pallas_call x1, Pallas kernels, local(): pl.pallas_call(kernel, out_shape=[pltpu.VMEM(shape, BF16) for shape in sh...  47.1 us
    unnamed x3, local copies, waits for them, and re-layouts  2.29 us

profile of v2, /device:TPU:1, one launch (start us, length us, event | category | flops | bytes accessed | tf_op | source)
XLA Modules:
  0.0 50.0 jit_solution(7076423637362305871)
XLA Ops:
  0.6 47.1 %shard_map.148 = (bf16[2,256,1024]{2,1,0:T(8,128)(2,1)S(1)}, bf16[512,256]{1,0:T(8,128)(2,1)S(1)}, bf16[4,4,1024]{2,1,0:T(4,128)(2,1)S(1)}) custom-call(s32[64]{0:T(128)} %plen_ref.1, s32[4]{0:T(128)} %adm_ref.1, s32[4]{0:T(128)} %clen_ref.1, f32[1,128]{1,0:T(1,128)} %constant.2.clone.freq_ref, f32[1,128]{1,0:T(1,128)} %bitcast.8, f32[1,128]{1,0:T(1,128)} %bitcast.9, ...), custom_call_target="tpu_custom_call" | custom-call | flops 10499999744 | bytes 25000000 | tf_op jit(solution)/shard_map/pallas_call | solution.py:560
  47.8 1.0 %copy.19 = bf16[2,256,1024]{2,1,0:T(8,128)(2,1)} copy(bf16[2,256,1024]{2,1,0:T(8,128)(2,1)S(1)} %get-tuple-element.9) | data formatting | bytes 2097152
  48.7 0.7 %copy.20 = bf16[1,64,8,256]{3,2,1,0:T(8,128)(2,1)} copy(bf16[1,64,8,256]{3,2,1,0:T(8,128)(2,1)S(1)} %bitcast.5) | data formatting | bytes 524288
  49.4 0.6 %copy.21 = bf16[4,4,1024]{2,1,0:T(4,128)(2,1)} copy(bf16[4,4,1024]{2,1,0:T(4,128)(2,1)S(1)} %get-tuple-element.11) | data formatting | bytes 65536

commit v3 on v2

--- a/solution.py
+++ b/solution.py
@@ -20,6 +20,7 @@
 CACHE = 512
 NS = 32
 NH = 4
+NB = WIDTH // HD
 EACH = LP // NS
 EPS = 1e-06
 THETA = 1000000.0
@@ -28,6 +29,7 @@
 LOG2E = 1.4426950408889634
 TILE = 256
 NT = WIDTH // TILE
+WIDE = 2 * TILE
 F32 = jnp.float32
 BF16 = jnp.bfloat16
 
@@ -104,6 +106,8 @@
     da_v,
     dpart_s,
     dpart_r,
+    dcol_s,
+    dcol_r,
     out_v,
     dout_v,
     small_sem,
@@ -118,6 +122,7 @@
     seq_rs,
     dpart_ss,
     dpart_rs,
+    dcol_sem,
 ):
     y = lax.axis_index("head")
     me = lax.axis_index("seq")
@@ -142,7 +147,7 @@
 
     def load_x(half, p):
         source = p * LP + half * HALF
-        target = half * (LP + ROWS) + p * HALF
+        target = half * LP + p * HALF
         return pltpu.make_async_copy(
             prompts.at[source : source + HALF], x_v.at[target : target + HALF], x_sem.at[half]
         )
@@ -168,10 +173,9 @@
 
     def load_o(k, j):
         start = lax.rem(y + k, NH) * WIDTH + j * TILE
-        sem = wo_sem.at[j if k in (2, 3) else NT + k]
+        sem = wo_sem.at[j // 2 if k in (2, 3) else 2 + k]
         return pltpu.make_async_copy(wo.at[:, rows(start, TILE)], wo_v.at[k, j], sem)
 
-    load_dec.start()
     load_k.start()
     load_v.start()
     load_x(0, 0).start()
@@ -210,27 +214,7 @@
         first, second = rotation(iota((HALF, HD), 0) + half * HALF, freq)
         tab_v[half, 0], tab_v[half, 1] = gained(first, second, q_gain)
         tab_v[half, 2], tab_v[half, 3] = gained(first, second, k_gain)
-    admitted = [adm[r] for r in range(SLOTS)]
-    handed_len = [plen[jnp.maximum(admitted[r], 0)] for r in range(SLOTS)]
-    is_new = [admitted[r] >= 0 for r in range(SLOTS)]
-    eff_len = [jnp.where(is_new[r], handed_len[r], clen[r]) for r in range(SLOTS)]
-
-    def per_slot(slot, values):
-        picked = jnp.full(slot.shape, values[0], jnp.int32)
-        for r in range(1, SLOTS):
-            picked = jnp.where(slot == r, values[r], picked)
-        return picked
-
-    token = iota((ROWS, HD), 0)
-    places = per_slot(token & (SLOTS - 1), eff_len) + (token >> 2)
-    first, second = rotation(places, freq)
-    dq_first, dq_second = gained(first, second, q_gain)
-    dk_first, dk_second = gained(first, second, k_gain)
-
-    load_dec.wait()
-    x_v[LP : LP + ROWS, :] = jnp.concatenate(
-        [dec_v[t].astype(F32) for t in range(STEPS)], axis=0
-    ).astype(BF16)
+    load_q(3).start()
 
     def finish_query(half, t, count):
         slot = lax.rem(t + 5, 6)
@@ -239,26 +223,29 @@
             for p in range(2):
                 one = normrot(mine[p * HALF : (p + 1) * HALF], tab_v[half, 0], tab_v[half, 1])
                 q_v[p, rows(slot * TILE + b * HD, HD), :] = one.astype(BF16)
-            if half == 0:
+            if half == 1:
                 one = normrot(mine[LP : LP + ROWS], dq_first, dq_second)
                 dq_v[rows((slot * 2 + b) * ROWS, ROWS), :] = one.astype(BF16)
 
     def multiply(half, after_keys=None):
-        start = half * (LP + ROWS)
-        count = LP if half else LP + ROWS
+        start = half * LP
+        count = LP + ROWS if half else LP
 
         def tile(t, carry):
             if half == 0:
                 landed(w_v.at[t], w_sem.at[t])
 
-                @pl.when(t < NT - 2)
+                @pl.when(t == 0)
                 def _():
-                    load_q(t + 3).start()
-
-                @pl.when(t < NT)
-                def _():
-                    load_o(2, t).start()
-                    load_o(3, t).start()
+                    load_q(4).start()
+
+                for jj in range(2):
+
+                    @pl.when(t == 1 + jj)
+                    def _(jj=jj):
+                        for j in (2 * jj, 2 * jj + 1):
+                            load_o(2, j).start()
+                            load_o(3, j).start()
 
             if after_keys is not None:
                 pl.when(t == 1)(after_keys)
@@ -277,57 +264,86 @@
             key = normrot(mine[:, 0:HD], tab_v[half, 2], tab_v[half, 3])
             kv_v[to, 0:HD] = key.astype(BF16)
             kv_v[to, HD : 2 * HD] = mine[:, HD : 2 * HD].astype(BF16)
-        if half == 0:
+        if half == 1:
             new = f_v[0, LP : LP + ROWS, :]
             dkv_v[...] = jnp.zeros_like(dkv_v)
             dkv_v[0:ROWS, 0:HD] = normrot(new[:, 0:HD], dk_first, dk_second).astype(BF16)
             dkv_v[0:ROWS, HD : 2 * HD] = new[:, HD : 2 * HD].astype(BF16)
 
-    def attend(half):
+    def attend(half, p):
         keys = (half + 1) * HALF
         at = iota((keys, HALF), 0)
         causal = at <= iota((keys, HALF), 1) + half * HALF
-        for p in range(2):
-            bias = jnp.where(causal & (at < plen[2 * me + p]), 0.0, NEG)
-            scores = dot_nt(kv_v[p * LP : p * LP + keys, 0:HD], q_v[p, 0 : GROUP * HALF])
-            scores = scores + jnp.concatenate([bias] * GROUP, axis=1)
-            top = jnp.max(scores, axis=0, keepdims=True)
-            expo = jnp.exp2((scores - top) * (SCALE * LOG2E))
-            weights = expo * (1.0 / jnp.sum(expo, axis=0, keepdims=True))
-            values = kv_v[p * LP : p * LP + keys, HD : 2 * HD].astype(F32).T.astype(BF16)
-            mixed = dot(values, weights.astype(BF16))
-            for head in range(GROUP):
-                one = mixed[:, head * HALF : (head + 1) * HALF].T.astype(BF16)
-                pa_v[half, p * HALF : (p + 1) * HALF, head * HD : (head + 1) * HD] = one
-
-    def part(slot, j):
+        bias = jnp.where(causal & (at < plen[2 * me + p]), 0.0, NEG)
+        mine = rows(p * LP, keys) if half else pl.ds(pl.multiple_of(p * LP, LP), keys)
+        scores = dot_nt(kv_v[mine, 0:HD], q_v[p, 0 : GROUP * HALF])
+        scores = scores + jnp.concatenate([bias] * GROUP, axis=1)
+        top = jnp.max(scores, axis=0, keepdims=True)
+        expo = jnp.exp2((scores - top) * (SCALE * LOG2E))
+        weights = expo * (1.0 / jnp.sum(expo, axis=0, keepdims=True))
+        values = kv_v[mine, HD : 2 * HD].astype(F32).T.astype(BF16)
+        mixed = dot(values, weights.astype(BF16))
+        for head in range(GROUP):
+            one = mixed[:, head * HALF : (head + 1) * HALF].T.astype(BF16)
+            pa_v[half, rows(p * HALF, HALF), head * HD : (head + 1) * HD] = one
+
+    def arrival(slot, i):
+        return {0: 0, 1: 4, 2: 8, 5: 12, 3: 16, 4: 17}[slot] + (0 if slot in (3, 4) else i)
+
+    def part(slot, i):
         to = right if slot in (0, 2, 3) else left
         return remote(
-            part_s.at[slot, j],
-            part_r.at[slot, j],
+            part_s.at[slot, i],
+            part_r.at[slot, i],
             part_ss.at[0],
-            part_rs.at[slot, 0 if slot in (3, 4) else j],
+            part_rs.at[arrival(slot, i)],
             head=to,
         )
 
-    def send_all(half, targets, tiles, far=None, load=False):
-        def tile(j, carry):
-            if load:
-                landed(wo_v.at[2:4, j], wo_sem.at[j])
+    def project(half, k, p, jj):
+        mine = pa_v[half, rows(p * HALF, HALF), :]
+        return jnp.concatenate([dot(mine, wo_v[k, 2 * jj + b]) for b in range(2)], axis=1)
+
+    def send(half, targets, p, jj, far=None):
+        i = p * 2 + jj
+        if far is not None:
+            landed(part_r.at[far, i], part_rs.at[arrival(far, i)])
+        values = [project(half, k, p, jj) for k, slot in targets]
+        for (k, slot), value in zip(targets, values):
             if far is not None:
-                landed(part_r.at[far, j], part_rs.at[far, j])
-            values = [dot(pa_v[half], wo_v[k, j]) for k, slot in targets]
-            for (k, slot), value in zip(targets, values):
-                if far is not None:
-                    value = value + part_r[far, j].astype(F32)
-                part_s[slot, j] = value.astype(BF16)
-                part(slot, j).start()
+                value = value + part_r[far, i].astype(F32)
+            part_s[slot, i] = value.astype(BF16)
+            part(slot, i).start()
+
+    def send_range(half, targets, first, last, far):
+        def tile(i, carry):
+            send(half, targets, i // 2, lax.rem(i, 2), far)
             return carry
 
-        lax.fori_loop(*tiles, tile, 0)
+        lax.fori_loop(first, last, tile, 0)
+
+    def attend_and_send(half, targets, load):
+        def prompt(p, carry):
+            attend(half, p)
+
+            def tile(jj, carry):
+                if load:
+
+                    @pl.when(p == 0)
+                    def _():
+                        landed(wo_v.at[2:4, pl.ds(2 * jj, 2)], wo_sem.at[jj])
+
+                send(half, targets, p, jj)
+                return carry
+
+            lax.fori_loop(0, 2, tile, 0)
+            return carry
+
+        lax.fori_loop(0, 2, prompt, 0)
 
     landed(x_v.at[0:LP], x_sem.at[0])
     multiply(0)
+    load_dec.start()
     load_x(1, 0).start()
     load_x(1, 1).start()
     for j in range(NT):
@@ -336,11 +352,31 @@
         load_o(0, j).start()
     load_cache.start()
     keys_values(0)
-    attend(0)
     pl.semaphore_wait(barrier, NS - 1 + NH - 1)
-    send_all(0, ((2, 0), (3, 4)), (0, NT), load=True)
-
-    landed(x_v.at[LP + ROWS : 2 * LP + ROWS], x_sem.at[1])
+    attend_and_send(0, ((2, 0), (3, 4)), True)
+
+    admitted = [adm[r] for r in range(SLOTS)]
+    handed_len = [plen[jnp.maximum(admitted[r], 0)] for r in range(SLOTS)]
+    is_new = [admitted[r] >= 0 for r in range(SLOTS)]
+    eff_len = [jnp.where(is_new[r], handed_len[r], clen[r]) for r in range(SLOTS)]
+
+    def per_slot(slot, values):
+        picked = jnp.full(slot.shape, values[0], jnp.int32)
+        for r in range(1, SLOTS):
+            picked = jnp.where(slot == r, values[r], picked)
+        return picked
+
+    token = iota((ROWS, HD), 0)
+    places = per_slot(token & (SLOTS - 1), eff_len) + (token >> 2)
+    first, second = rotation(places, freq)
+    dq_first, dq_second = gained(first, second, q_gain)
+    dk_first, dk_second = gained(first, second, k_gain)
+
+    landed(x_v.at[LP : 2 * LP], x_sem.at[1])
+    load_dec.wait()
+    x_v[2 * LP : 2 * LP + ROWS, :] = jnp.concatenate(
+        [dec_v[t].astype(F32) for t in range(STEPS)], axis=0
+    ).astype(BF16)
     def hand(i, way):
         other = lax.rem(me + i, NS)
         return remote(
@@ -366,9 +402,8 @@
         lax.fori_loop(1, NS, hand_start, 0)
 
     multiply(1, hand_over)
-    attend(1)
-    landed(wo_v.at[1], wo_sem.at[NT + 1])
-    send_all(1, ((1, 3), (2, 1)), (0, NT))
+    landed(wo_v.at[1], wo_sem.at[3])
+    attend_and_send(1, ((1, 3), (2, 1)), False)
     load_cache.wait()
 
     landed(hand_v.at[0 : (NS - 1) * 16], seq_rs.at[0])
@@ -435,16 +470,16 @@
 
     lax.fori_loop(1, NS, soft_start, 0)
 
-    send_all(0, ((1, 2),), (0, NT), far=0)
-
-    landed(wo_v.at[0], wo_sem.at[NT])
-
-    def own(j, carry):
-        own_v[0, j] = dot(pa_v[0], wo_v[0, j])
-        own_v[1, j] = dot(pa_v[1], wo_v[0, j])
+    send_range(0, ((1, 2),), 0, 1, 0)
+
+    landed(wo_v.at[0], wo_sem.at[2])
+
+    def own(i, carry):
+        for half in range(2):
+            own_v[half, i] = project(half, 0, i // 2, lax.rem(i, 2))
         return carry
 
-    lax.fori_loop(0, NT, own, 0)
+    lax.fori_loop(0, 4, own, 0)
 
     landed(soft_r.at[0 : (NS - 1) * 8], seq_rs.at[1])
     joined = []
@@ -473,11 +508,13 @@
     lax.fori_loop(1, NS, join_start, 0)
 
 
-    send_all(1, ((3, 5),), (0, NT - 1), far=1)
+    send_range(1, ((3, 5),), 0, 1, 1)
     landed(join_r.at[0 : (NS - 1) * 8], seq_rs.at[2])
     for head in range(GROUP):
         start = (head % 2) * ROWS * 8 + head // 2
         da_v[:, head * HD : (head + 1) * HD] = join_r[pl.ds(start, ROWS, stride=8), :].astype(BF16)
+
+    block = lax.rem(me, NB)
 
     def dpart(k):
         return remote(
@@ -489,52 +526,88 @@
         )
 
     def dec_project(k):
-        return jnp.concatenate([dot(da_v[...], wo_v[k, j]) for j in range(NT)], axis=1)
+        lanes = rows(lax.rem(block, 2) * HD, HD)
+        return dot(da_v[...], wo_v[k, block // 2, :, lanes])
 
     for k in (2, 1, 3):
         dpart_s[k] = dec_project(k).astype(BF16)
         dpart(k).start()
     dec_own = dec_project(0)
 
-    send_all(1, ((3, 5),), (NT - 1, NT), far=1)
+    def mixed(i, carry):
+        send(0, ((1, 2),), i // 2, lax.rem(i, 2), 0)
+        send(1, ((3, 5),), i // 2, lax.rem(i, 2), 1)
+        return carry
+
+    lax.fori_loop(1, 4, mixed, 0)
+
+    landed(dpart_r.at[1:NH], dpart_rs.at[0])
+    for k in (1, 3, 2):
+        dec_own = dec_own + dpart_r[k].astype(F32)
+    dcol_s[...] = dec_own
+    dcol_r[block] = dec_own
+
+    def dcol(i):
+        other = lax.rem(block + i, NB)
+        return remote(
+            dcol_s, dcol_r.at[block], dcol_sem.at[0], dcol_sem.at[1], seq=me - block + other
+        )
+
+    def dcol_start(i, carry):
+        dcol(i).start()
+        return carry
+
+    lax.fori_loop(1, NB, dcol_start, 0)
     landed(hand_v.at[0 : (NS - 1) * 16], seq_ss.at[0])
     landed(soft_r.at[0 : (NS - 1) * 8], seq_ss.at[1])
     landed(join_r.at[0 : (NS - 1) * 8], seq_ss.at[2])
     save_hand.wait()
 
-    landed(part_r.at[3], part_rs.at[3, 0])
-    landed(part_r.at[4], part_rs.at[4, 0])
-
-    def finish(j, carry):
+    landed(part_r.at[3], part_rs.at[arrival(3, 0)])
+    landed(part_r.at[4], part_rs.at[arrival(4, 0)])
+
+    def finish(i, carry):
+        landed(part_r.at[2, i], part_rs.at[arrival(2, i)])
+        landed(part_r.at[5, i], part_rs.at[arrival(5, i)])
+        p, jj = i // 2, lax.rem(i, 2)
         for half in range(2):
-            late = 5 if half else 2
-            landed(part_r.at[late, j], part_rs.at[late, j])
-        for half in range(2):
-            value = own_v[half, j] + part_r[2 + half, j].astype(F32)
-            value = (value + part_r[4 + half, j].astype(F32)).astype(BF16)
-            for p in range(2):
-                out_v[half, j, p] = value[p * HALF : (p + 1) * HALF]
+            value = own_v[half, i] + part_r[2 + half, i].astype(F32)
+            out_v[half, i] = (value + part_r[4 + half, i].astype(F32)).astype(BF16)
             pltpu.make_async_copy(
-                out_v.at[half, j],
-                out.at[:, half * HALF : (half + 1) * HALF, rows(j * TILE, TILE)],
+                out_v.at[half, i],
+                out.at[p, half * HALF : (half + 1) * HALF, rows(jj * WIDE, WIDE)],
                 out_sem.at[2],
             ).start()
         return carry
 
-    lax.fori_loop(0, NT, finish, 0)
-
-    landed(dpart_r.at[1:NH], dpart_rs.at[0])
-    for k in (1, 3, 2):
-        dec_own = dec_own + dpart_r[k].astype(F32)
-    for t in range(STEPS):
-        dout_v[t] = dec_own[t * SLOTS : (t + 1) * SLOTS].astype(BF16)
-    save_dec = pltpu.make_async_copy(dout_v, dec_out, out_sem.at[1])
-    save_dec.start()
+    def save_decoded():
+        landed(dcol_r.at[0 : NB - 1], dcol_sem.at[1])
+        for b in range(NB):
+            for t in range(STEPS):
+                mine = dcol_r[b, t * SLOTS : (t + 1) * SLOTS, :]
+                dout_v[t, :, b * HD : (b + 1) * HD] = mine.astype(BF16)
+        pltpu.make_async_copy(dout_v, dec_out, out_sem.at[1]).start()
+
+    lax.fori_loop(0, 3, finish, 0)
+    save_decoded()
+    lax.fori_loop(3, 4, finish, 0)
 
     landed(dpart_s.at[1:NH], dpart_ss.at[0])
     landed(part_s, part_ss.at[0])
     landed(out_v, out_sem.at[2])
-    save_dec.wait()
+    landed(dout_v, out_sem.at[1])
+    landed(dcol_r.at[0 : NB - 1], dcol_sem.at[0])
+
+
+def store(out_v, hand_v, dec_v, out, handed, dec_out, sem):
+    copies = [
+        pltpu.make_async_copy(source, target, sem.at[i])
+        for i, (source, target) in enumerate([(out_v, out), (hand_v, handed), (dec_v, dec_out)])
+    ]
+    for copy in copies:
+        copy.start()
+    for copy in copies:
+        copy.wait()
 
 
 def local(
@@ -557,7 +630,7 @@
     hbm = pl.BlockSpec(memory_space=pl.ANY)
     dma = pltpu.SemaphoreType.DMA
     shapes = [(2, LP, WIDTH), (2 * LP, 2 * HD), (STEPS, SLOTS, WIDTH)]
-    out, handed, decoded = pl.pallas_call(
+    results = pl.pallas_call(
         kernel,
         out_shape=[pltpu.VMEM(shape, BF16) for shape in shapes],
         in_specs=[hbm] * 13,
@@ -581,30 +654,33 @@
             pltpu.VMEM(((GROUP + 4) * ROWS, HD), BF16),
             pltpu.VMEM((HD, 2 * HD), BF16),
             pltpu.VMEM((2, LP, WIDTH), BF16),
-            pltpu.VMEM((6, NT, LP, TILE), BF16),
-            pltpu.VMEM((6, NT, LP, TILE), BF16),
-            pltpu.VMEM((2, NT, LP, TILE), F32),
+            pltpu.VMEM((6, 4, HALF, WIDE), BF16),
+            pltpu.VMEM((6, 4, HALF, WIDE), BF16),
+            pltpu.VMEM((2, 4, HALF, WIDE), F32),
             pltpu.VMEM((NS * 8, HD), F32),
             pltpu.VMEM((NS * 8, HD), F32),
             pltpu.VMEM((8, HD), F32),
             pltpu.VMEM((NS * 8, HD), F32),
             pltpu.VMEM((ROWS, WIDTH), BF16),
-            pltpu.VMEM((NH, ROWS, WIDTH), BF16),
-            pltpu.VMEM((NH, ROWS, WIDTH), BF16),
-            pltpu.VMEM((2, NT, 2, HALF, TILE), BF16),
+            pltpu.VMEM((NH, ROWS, HD), BF16),
+            pltpu.VMEM((NH, ROWS, HD), BF16),
+            pltpu.VMEM((ROWS, HD), F32),
+            pltpu.VMEM((NB, ROWS, HD), F32),
+            pltpu.VMEM((2, 4, HALF, WIDE), BF16),
             pltpu.VMEM((STEPS, SLOTS, WIDTH), BF16),
             dma((4,)),
             dma((2,)),
             dma((2,)),
             dma((1 + NT,)),
-            dma((NT + 2,)),
+            dma((4,)),
             dma((3,)),
             dma((1,)),
-            dma((6, NT)),
+            dma((18,)),
             dma((3,)),
             dma((3,)),
             dma((1,)),
             dma((1,)),
+            dma((2,)),
         ],
         compiler_params=pltpu.CompilerParams(
             collective_id=0, has_side_effects=True, vmem_limit_bytes=56 * 2**20
@@ -627,6 +703,14 @@
         w_out,
         cache_kv.reshape(SLOTS * CACHE, 2 * HD),
     )
+    out, handed, decoded = pl.pallas_call(
+        store,
+        out_shape=[jax.ShapeDtypeStruct(shape, BF16) for shape in shapes],
+        in_specs=[hbm] * 3,
+        out_specs=[hbm] * 3,
+        scratch_shapes=[dma((3,))],
+        compiler_params=pltpu.CompilerParams(vmem_limit_bytes=2**20),
+    )(*results)
     return (
         out,
         handed.reshape(1, 2 * NS, EACH, 2 * HD),

time: 50.3 us -> 48.8 us (0.970)
  local copies, waits for them, and re-layouts: 2.29 us -> 0 us
  Pallas kernels: 47.1 us -> 48 us
    unnamed x3 -> x0, local copies, waits for them, and re-layouts: 2.29 us -> none
    pallas_call x0 -> x1, Pallas kernels: none -> 1.08 us  [local(): pl.pallas_call(store, out_shape=[jax.ShapeDtypeStruct(shape, BF16) for sh...]
where the time goes in v3:
time: 48.8 us; the launch traced here: 48.7 us
  Pallas kernels  48 us (98%)
  between operations  0.64 us (1%)
    pallas_call x1, Pallas kernels, local(): pl.pallas_call(kernel, out_shape=[pltpu.VMEM(shape, BF16) for shape in sh...  46.9 us
    pallas_call x1, Pallas kernels, local(): pl.pallas_call(store, out_shape=[jax.ShapeDtypeStruct(shape, BF16) for sh...  1.08 us

profile of v3, /device:TPU:1, one launch (start us, length us, event | category | flops | bytes accessed | tf_op | source)
XLA Modules:
  0.0 48.7 jit_solution(2700020619082584290)
XLA Ops:
  0.6 46.9 %shard_map.148 = (bf16[2,256,1024]{2,1,0:T(8,128)(2,1)S(1)}, bf16[512,256]{1,0:T(8,128)(2,1)S(1)}, bf16[4,4,1024]{2,1,0:T(4,128)(2,1)S(1)}) custom-call(s32[64]{0:T(128)} %plen_ref.1, s32[4]{0:T(128)} %adm_ref.1, s32[4]{0:T(128)} %clen_ref.1, f32[1,128]{1,0:T(1,128)} %constant.2.clone.freq_ref, f32[1,128]{1,0:T(1,128)} %bitcast.8, f32[1,128]{1,0:T(1,128)} %bitcast.9, ...), custom_call_target="tpu_custom_call" | custom-call | flops 10499999744 | bytes 25000000 | tf_op jit(solution)/shard_map/pallas_call | solution.py:633
  47.6 1.1 %shard_map.149 = (bf16[2,256,1024]{2,1,0:T(8,128)(2,1)}, bf16[512,256]{1,0:T(8,128)(2,1)}, bf16[4,4,1024]{2,1,0:T(4,128)(2,1)}) custom-call(bf16[2,256,1024]{2,1,0:T(8,128)(2,1)S(1)} %get-tuple-element.9.out_v, bf16[512,256]{1,0:T(8,128)(2,1)S(1)} %get-tuple-element.10.hand_v, bf16[4,4,1024]{2,1,0:T(4,128)(2,1)S(1)} %get-tuple-element.11.dec_v), custom_call_target="tpu_custom_call" | custom-call | tf_op jit(solution)/shard_map/pallas_call | solution.py:706

commit v4 on v3

--- a/solution.py
+++ b/solution.py
@@ -20,7 +20,6 @@
 CACHE = 512
 NS = 32
 NH = 4
-NB = WIDTH // HD
 EACH = LP // NS
 EPS = 1e-06
 THETA = 1000000.0
@@ -103,11 +102,8 @@
     soft_r,
     join_s,
     join_r,
-    da_v,
     dpart_s,
     dpart_r,
-    dcol_s,
-    dcol_r,
     out_v,
     dout_v,
     small_sem,
@@ -122,7 +118,6 @@
     seq_rs,
     dpart_ss,
     dpart_rs,
-    dcol_sem,
 ):
     y = lax.axis_index("head")
     me = lax.axis_index("seq")
@@ -149,7 +144,7 @@
         source = p * LP + half * HALF
         target = half * LP + p * HALF
         return pltpu.make_async_copy(
-            prompts.at[source : source + HALF], x_v.at[target : target + HALF], x_sem.at[half]
+            prompts.at[source : source + HALF], x_v.at[target : target + HALF], x_sem.at[half + (p if half == 0 else 1)]
         )
 
     small = [
@@ -177,11 +172,11 @@
         return pltpu.make_async_copy(wo.at[:, rows(start, TILE)], wo_v.at[k, j], sem)
 
     load_k.start()
+    load_x(0, 0).start()
     load_v.start()
-    load_x(0, 0).start()
-    load_x(0, 1).start()
     for load in small:
         load.start()
+    load_q(1).start()
 
     barrier = pltpu.get_barrier_semaphore()
 
@@ -203,7 +198,6 @@
         )
     lax.fori_loop(1, NS, greet, 0)
 
-    load_q(1).start()
     load_q(2).start()
 
     landed(row_v, small_sem.at[0])
@@ -216,23 +210,30 @@
         tab_v[half, 2], tab_v[half, 3] = gained(first, second, k_gain)
     load_q(3).start()
 
-    def finish_query(half, t, count):
+    def finish_query(half, p, t, base):
         slot = lax.rem(t + 5, 6)
         for b in range(TILE // HD):
-            mine = f_v[t, 0:count, b * HD : (b + 1) * HD]
-            for p in range(2):
-                one = normrot(mine[p * HALF : (p + 1) * HALF], tab_v[half, 0], tab_v[half, 1])
-                q_v[p, rows(slot * TILE + b * HD, HD), :] = one.astype(BF16)
-            if half == 1:
-                one = normrot(mine[LP : LP + ROWS], dq_first, dq_second)
-                dq_v[rows((slot * 2 + b) * ROWS, ROWS), :] = one.astype(BF16)
-
-    def multiply(half, after_keys=None):
-        start = half * LP
-        count = LP + ROWS if half else LP
-
+            mine = f_v[t, base : base + HALF, b * HD : (b + 1) * HD]
+            one = normrot(mine, tab_v[half, 0], tab_v[half, 1])
+            q_v[p, rows(slot * TILE + b * HD, HD), :] = one.astype(BF16)
+
+    def finish_token(t):
+        slot = lax.rem(t + 5, 6)
+        for b in range(TILE // HD):
+            mine = f_v[t, LP : LP + ROWS, b * HD : (b + 1) * HD]
+            one = normrot(mine, dq_first, dq_second)
+            dq_v[rows((slot * 2 + b) * ROWS, ROWS), :] = one.astype(BF16)
+
+    def keys_values(half, p, base):
+        mine = f_v[0, base : base + HALF, :]
+        to = rows(p * LP + half * HALF, HALF)
+        kv_v[to, 0:HD] = normrot(mine[:, 0:HD], tab_v[half, 2], tab_v[half, 3]).astype(BF16)
+        kv_v[to, HD : 2 * HD] = mine[:, HD : 2 * HD].astype(BF16)
+
+    def multiply_first(p):
         def tile(t, carry):
-            if half == 0:
+            @pl.when(p == 0)
+            def _():
                 landed(w_v.at[t], w_sem.at[t])
 
                 @pl.when(t == 0)
@@ -247,28 +248,32 @@
                             load_o(2, j).start()
                             load_o(3, j).start()
 
-            if after_keys is not None:
-                pl.when(t == 1)(after_keys)
-
-            finish_query(half, lax.rem(t + 5, 6), count)
-            f_v[t, 0:count, :] = dot(x_v[start : start + count, :], w_v[t])
+                @pl.when(t == 2)
+                def _():
+                    load_x(0, 1).start()
+
+            finish_query(0, p, lax.rem(t + 5, 6), 0)
+            f_v[t, 0:HALF, :] = dot(x_v[rows(p * HALF, HALF), :], w_v[t])
             return carry
 
         lax.fori_loop(0, 1 + NT, tile, 0)
-        finish_query(half, NT, count)
-
-    def keys_values(half):
-        for p in range(2):
-            mine = f_v[0, p * HALF : (p + 1) * HALF, :]
-            to = slice(p * LP + half * HALF, p * LP + (half + 1) * HALF)
-            key = normrot(mine[:, 0:HD], tab_v[half, 2], tab_v[half, 3])
-            kv_v[to, 0:HD] = key.astype(BF16)
-            kv_v[to, HD : 2 * HD] = mine[:, HD : 2 * HD].astype(BF16)
-        if half == 1:
-            new = f_v[0, LP : LP + ROWS, :]
-            dkv_v[...] = jnp.zeros_like(dkv_v)
-            dkv_v[0:ROWS, 0:HD] = normrot(new[:, 0:HD], dk_first, dk_second).astype(BF16)
-            dkv_v[0:ROWS, HD : 2 * HD] = new[:, HD : 2 * HD].astype(BF16)
+        finish_query(0, p, NT, 0)
+        keys_values(0, p, 0)
+
+    def multiply_second(after_keys):
+        def finish(t):
+            for p in range(2):
+                finish_query(1, p, t, p * HALF)
+            finish_token(t)
+
+        def tile(t, carry):
+            pl.when(t == 1)(after_keys)
+            finish(lax.rem(t + 5, 6))
+            f_v[t] = dot(x_v[LP : 2 * LP + ROWS, :], w_v[t])
+            return carry
+
+        lax.fori_loop(0, 1 + NT, tile, 0)
+        finish(NT)
 
     def attend(half, p):
         keys = (half + 1) * HALF
@@ -288,7 +293,10 @@
             pa_v[half, rows(p * HALF, HALF), head * HD : (head + 1) * HD] = one
 
     def arrival(slot, i):
-        return {0: 0, 1: 4, 2: 8, 5: 12, 3: 16, 4: 17}[slot] + (0 if slot in (3, 4) else i)
+        return {0: 0, 1: 1 + i // 3, 2: 3 + i // 3, 5: 5 + i // 3, 3: 7, 4: 8}[slot]
+
+    def arrived(slot, first, last):
+        landed(part_r.at[slot, first:last], part_rs.at[arrival(slot, first)])
 
     def part(slot, i):
         to = right if slot in (0, 2, 3) else left
@@ -306,8 +314,6 @@
 
     def send(half, targets, p, jj, far=None):
         i = p * 2 + jj
-        if far is not None:
-            landed(part_r.at[far, i], part_rs.at[arrival(far, i)])
         values = [project(half, k, p, jj) for k, slot in targets]
         for (k, slot), value in zip(targets, values):
             if far is not None:
@@ -315,45 +321,51 @@
             part_s[slot, i] = value.astype(BF16)
             part(slot, i).start()
 
-    def send_range(half, targets, first, last, far):
-        def tile(i, carry):
-            send(half, targets, i // 2, lax.rem(i, 2), far)
+    def first_half(p, carry):
+        @pl.when(p == 1)
+        def _():
+            landed(x_v.at[HALF:LP], x_sem.at[1])
+
+        multiply_first(p)
+        attend(0, p)
+
+        def tile(jj, carry):
+            @pl.when(p == 0)
+            def _():
+                landed(wo_v.at[2:4, pl.ds(2 * jj, 2)], wo_sem.at[jj])
+
+                @pl.when(jj == 0)
+                def _():
+                    pl.semaphore_wait(barrier, NS - 1 + NH - 1)
+
+            send(0, ((2, 0), (3, 4)), p, jj)
             return carry
 
-        lax.fori_loop(first, last, tile, 0)
-
-    def attend_and_send(half, targets, load):
-        def prompt(p, carry):
-            attend(half, p)
-
-            def tile(jj, carry):
-                if load:
-
-                    @pl.when(p == 0)
-                    def _():
-                        landed(wo_v.at[2:4, pl.ds(2 * jj, 2)], wo_sem.at[jj])
-
-                send(half, targets, p, jj)
-                return carry
-
-            lax.fori_loop(0, 2, tile, 0)
+        lax.fori_loop(0, 2, tile, 0)
+
+        @pl.when(p == 0)
+        def _():
+            load_dec.start()
+            load_x(1, 0).start()
+            load_x(1, 1).start()
+            for k in (1, 0):
+                for j in range(NT):
+                    load_o(k, j).start()
+            load_cache.start()
+
+        return carry
+
+    def second_half(p):
+        attend(1, p)
+
+        def tile(jj, carry):
+            send(1, ((1, 3), (2, 1)), p, jj)
             return carry
 
-        lax.fori_loop(0, 2, prompt, 0)
-
-    landed(x_v.at[0:LP], x_sem.at[0])
-    multiply(0)
-    load_dec.start()
-    load_x(1, 0).start()
-    load_x(1, 1).start()
-    for j in range(NT):
-        load_o(1, j).start()
-    for j in range(NT):
-        load_o(0, j).start()
-    load_cache.start()
-    keys_values(0)
-    pl.semaphore_wait(barrier, NS - 1 + NH - 1)
-    attend_and_send(0, ((2, 0), (3, 4)), True)
+        lax.fori_loop(0, 2, tile, 0)
+
+    landed(x_v.at[0:HALF], x_sem.at[0])
+    lax.fori_loop(0, 2, first_half, 0)
 
     admitted = [adm[r] for r in range(SLOTS)]
     handed_len = [plen[jnp.maximum(admitted[r], 0)] for r in range(SLOTS)]
@@ -372,7 +384,7 @@
     dq_first, dq_second = gained(first, second, q_gain)
     dk_first, dk_second = gained(first, second, k_gain)
 
-    landed(x_v.at[LP : 2 * LP], x_sem.at[1])
+    landed(x_v.at[LP : 2 * LP], x_sem.at[2])
     load_dec.wait()
     x_v[2 * LP : 2 * LP + ROWS, :] = jnp.concatenate(
         [dec_v[t].astype(F32) for t in range(STEPS)], axis=0
@@ -388,7 +400,12 @@
         )
 
     def hand_over():
-        keys_values(1)
+        for p in range(2):
+            keys_values(1, p, p * HALF)
+        new = f_v[0, LP : LP + ROWS, :]
+        dkv_v[...] = jnp.zeros_like(dkv_v)
+        dkv_v[0:ROWS, 0:HD] = normrot(new[:, 0:HD], dk_first, dk_second).astype(BF16)
+        dkv_v[0:ROWS, HD : 2 * HD] = new[:, HD : 2 * HD].astype(BF16)
         place = iota((2 * LP, 2 * LP), 0)
         source = (((place >> 3) & 1) << 8) + ((place & 7) << 5) + (place >> 4)
         pick = jnp.where(source == iota((2 * LP, 2 * LP), 1), 1.0, 0.0).astype(BF16)
@@ -401,9 +418,9 @@
 
         lax.fori_loop(1, NS, hand_start, 0)
 
-    multiply(1, hand_over)
+    multiply_second(hand_over)
     landed(wo_v.at[1], wo_sem.at[3])
-    attend_and_send(1, ((1, 3), (2, 1)), False)
+    second_half(0)
     load_cache.wait()
 
     landed(hand_v.at[0 : (NS - 1) * 16], seq_rs.at[0])
@@ -449,9 +466,11 @@
         total = total + jnp.sum(expo, axis=-1, keepdims=True)
         acc = acc + dot(expo.astype(BF16), v)
     state = jnp.where(iota((heads, HD), 1) < HD // 2, top, total)
-    for q in range(heads // NS):
-        soft_s[pl.ds(q, NS, stride=8), :] = acc[q * NS : (q + 1) * NS, :]
-        soft_s[pl.ds(q + 4, NS, stride=8), :] = state[q * NS : (q + 1) * NS, :]
+    for head in range(GROUP):
+        at = pl.ds(8 * (head // 4) + head % 4, ROWS, stride=16)
+        soft_s[at, :] = acc[head * ROWS : (head + 1) * ROWS, :]
+        also = pl.ds(8 * (head // 4) + head % 4 + 4, ROWS, stride=16)
+        soft_s[also, :] = state[head * ROWS : (head + 1) * ROWS, :]
     soft_r[rows(me * 8, 8), :] = soft_s[rows(me * 8, 8), :]
 
     def soft(i, way):
@@ -469,8 +488,7 @@
         return carry
 
     lax.fori_loop(1, NS, soft_start, 0)
-
-    send_range(0, ((1, 2),), 0, 1, 0)
+    second_half(1)
 
     landed(wo_v.at[0], wo_sem.at[2])
 
@@ -489,86 +507,73 @@
         tops = both[:, 0:1]
         weight = jnp.exp2((tops - jnp.max(tops, axis=0, keepdims=True)) * (SCALE * LOG2E))
         whole = jnp.sum(weight * both[:, HD // 2 : HD // 2 + 1], axis=0, keepdims=True)
-        joined.append(jnp.sum(weight * sums, axis=0, keepdims=True) / whole)
-    for q in range(heads // NS):
-        join_s[q : q + 1, :] = joined[q]
-        join_s[q + 4 : q + 5, :] = joined[q]
-    join_r[rows(me * 8, 8), :] = join_s[...]
-
-    def join(i, way):
-        other = lax.rem(me + i, NS)
+        joined.append((jnp.sum(weight * sums, axis=0, keepdims=True) / whole).astype(BF16))
+    token_row = jnp.broadcast_to(jnp.concatenate(joined, axis=1).astype(F32), (16, WIDTH // 2))
+    token_row = token_row.astype(BF16)
+
+    core = lax.rem(me, 2)
+
+    def dpart(k, e):
         return remote(
-            join_s, join_r.at[rows(way * 8, 8)], seq_ss.at[2], seq_rs.at[2], seq=other
-        )
-
-    def join_start(i, carry):
-        join(i, me).start()
-        return carry
-
-    lax.fori_loop(1, NS, join_start, 0)
-
-
-    send_range(1, ((3, 5),), 0, 1, 1)
-    landed(join_r.at[0 : (NS - 1) * 8], seq_rs.at[2])
-    for head in range(GROUP):
-        start = (head % 2) * ROWS * 8 + head // 2
-        da_v[:, head * HD : (head + 1) * HD] = join_r[pl.ds(start, ROWS, stride=8), :].astype(BF16)
-
-    block = lax.rem(me, NB)
-
-    def dpart(k):
-        return remote(
-            dpart_s.at[k],
-            dpart_r.at[k],
+            dpart_s.at[2 * k + e],
+            dpart_r.at[2 * k + e],
             dpart_ss.at[0],
             dpart_rs.at[0],
             head=lax.rem(y + k, NH),
-        )
-
-    def dec_project(k):
-        lanes = rows(lax.rem(block, 2) * HD, HD)
-        return dot(da_v[...], wo_v[k, block // 2, :, lanes])
-
-    for k in (2, 1, 3):
-        dpart_s[k] = dec_project(k).astype(BF16)
-        dpart(k).start()
-    dec_own = dec_project(0)
+            seq=me + e * (1 - 2 * core),
+        )
+
+    for k in (2, 1, 3, 0):
+        for e in range(2):
+            side = core + e * (1 - 2 * core)
+            for b in range(2):
+                tile = wo_v[k, 2 * side + b, rows(core * (WIDTH // 2), WIDTH // 2), :]
+                value = dot(token_row, tile)[0:1]
+                for lanes in range(2):
+                    one = value[:, lanes * HD : (lanes + 1) * HD]
+                    row = 2 * b + lanes
+                    dpart_s[2 * k + e, row : row + 1, :] = one
+                    dpart_s[2 * k + e, row + 4 : row + 5, :] = one
+            if (k, e) != (0, 0):
+                dpart(k, e).start()
+
+    arrived(0, 0, 4)
+    arrived(1, 0, 3)
 
     def mixed(i, carry):
         send(0, ((1, 2),), i // 2, lax.rem(i, 2), 0)
         send(1, ((3, 5),), i // 2, lax.rem(i, 2), 1)
         return carry
 
-    lax.fori_loop(1, 4, mixed, 0)
-
-    landed(dpart_r.at[1:NH], dpart_rs.at[0])
-    for k in (1, 3, 2):
-        dec_own = dec_own + dpart_r[k].astype(F32)
-    dcol_s[...] = dec_own
-    dcol_r[block] = dec_own
-
-    def dcol(i):
-        other = lax.rem(block + i, NB)
-        return remote(
-            dcol_s, dcol_r.at[block], dcol_sem.at[0], dcol_sem.at[1], seq=me - block + other
-        )
-
-    def dcol_start(i, carry):
-        dcol(i).start()
+    lax.fori_loop(0, 3, mixed, 0)
+    arrived(1, 3, 4)
+    mixed(3, 0)
+
+    landed(dpart_r.at[1 : 2 * NH], dpart_rs.at[0])
+    total = dpart_s[0]
+    for n in range(1, 2 * NH):
+        total = total + dpart_r[n]
+    join_s[...] = total
+    join_r[rows(me * 8, 8), :] = total
+
+    def join(i, way):
+        other = lax.rem(me + i, NS)
+        return remote(join_s, join_r.at[rows(way * 8, 8)], seq_ss.at[2], seq_rs.at[2], seq=other)
+
+    def join_start(i, carry):
+        join(i, me).start()
         return carry
 
-    lax.fori_loop(1, NB, dcol_start, 0)
+    lax.fori_loop(1, NS, join_start, 0)
+
     landed(hand_v.at[0 : (NS - 1) * 16], seq_ss.at[0])
     landed(soft_r.at[0 : (NS - 1) * 8], seq_ss.at[1])
-    landed(join_r.at[0 : (NS - 1) * 8], seq_ss.at[2])
     save_hand.wait()
 
-    landed(part_r.at[3], part_rs.at[arrival(3, 0)])
-    landed(part_r.at[4], part_rs.at[arrival(4, 0)])
+    arrived(3, 0, 4)
+    arrived(4, 0, 4)
 
     def finish(i, carry):
-        landed(part_r.at[2, i], part_rs.at[arrival(2, i)])
-        landed(part_r.at[5, i], part_rs.at[arrival(5, i)])
         p, jj = i // 2, lax.rem(i, 2)
         for half in range(2):
             value = own_v[half, i] + part_r[2 + half, i].astype(F32)
@@ -581,22 +586,27 @@
         return carry
 
     def save_decoded():
-        landed(dcol_r.at[0 : NB - 1], dcol_sem.at[1])
-        for b in range(NB):
+        landed(join_r.at[0 : (NS - 1) * 8], seq_rs.at[2])
+        for b in range(GROUP):
+            mine = join_r[pl.ds(8 * (b // 4) + b % 4, ROWS, stride=16), :]
             for t in range(STEPS):
-                mine = dcol_r[b, t * SLOTS : (t + 1) * SLOTS, :]
-                dout_v[t, :, b * HD : (b + 1) * HD] = mine.astype(BF16)
+                one = mine[t * SLOTS : (t + 1) * SLOTS, :]
+                dout_v[t, :, b * HD : (b + 1) * HD] = one.astype(BF16)
         pltpu.make_async_copy(dout_v, dec_out, out_sem.at[1]).start()
 
+    arrived(2, 0, 3)
+    arrived(5, 0, 3)
     lax.fori_loop(0, 3, finish, 0)
     save_decoded()
-    lax.fori_loop(3, 4, finish, 0)
-
-    landed(dpart_s.at[1:NH], dpart_ss.at[0])
+    arrived(2, 3, 4)
+    arrived(5, 3, 4)
+    finish(3, 0)
+
+    landed(dpart_s.at[1 : 2 * NH], dpart_ss.at[0])
+    landed(join_r.at[0 : (NS - 1) * 8], seq_ss.at[2])
     landed(part_s, part_ss.at[0])
     landed(out_v, out_sem.at[2])
     landed(dout_v, out_sem.at[1])
-    landed(dcol_r.at[0 : NB - 1], dcol_sem.at[0])
 
 
 def store(out_v, hand_v, dec_v, out, handed, dec_out, sem):
@@ -661,26 +671,22 @@
             pltpu.VMEM((NS * 8, HD), F32),
             pltpu.VMEM((8, HD), F32),
             pltpu.VMEM((NS * 8, HD), F32),
-            pltpu.VMEM((ROWS, WIDTH), BF16),
-            pltpu.VMEM((NH, ROWS, HD), BF16),
-            pltpu.VMEM((NH, ROWS, HD), BF16),
-            pltpu.VMEM((ROWS, HD), F32),
-            pltpu.VMEM((NB, ROWS, HD), F32),
+            pltpu.VMEM((2 * NH, 8, HD), F32),
+            pltpu.VMEM((2 * NH, 8, HD), F32),
             pltpu.VMEM((2, 4, HALF, WIDE), BF16),
             pltpu.VMEM((STEPS, SLOTS, WIDTH), BF16),
             dma((4,)),
-            dma((2,)),
+            dma((3,)),
             dma((2,)),
             dma((1 + NT,)),
             dma((4,)),
             dma((3,)),
             dma((1,)),
-            dma((18,)),
+            dma((9,)),
             dma((3,)),
             dma((3,)),
             dma((1,)),
             dma((1,)),
-            dma((2,)),
         ],
         compiler_params=pltpu.CompilerParams(
             collective_id=0, has_side_effects=True, vmem_limit_bytes=56 * 2**20

time: 48.8 us -> 48.3 us (0.990)
  Pallas kernels: 48 us -> 47.5 us
    pallas_call x1, Pallas kernels: 46.9 us -> 46.4 us  [local(): pl.pallas_call(kernel, out_shape=[pltpu.VMEM(shape, BF16) for shape in sh...]
where the time goes in v4:
time: 48.3 us; the launch traced here: 48.1 us
  Pallas kernels  47.5 us (98%)
  between operations  0.64 us (1%)
    pallas_call x1, Pallas kernels, local(): pl.pallas_call(kernel, out_shape=[pltpu.VMEM(shape, BF16) for shape in sh...  46.4 us
    pallas_call x1, Pallas kernels, local(): pl.pallas_call(store, out_shape=[jax.ShapeDtypeStruct(shape, BF16) for sh...  1.08 us

profile of v4, /device:TPU:1, one launch (start us, length us, event | category | flops | bytes accessed | tf_op | source)
XLA Modules:
  0.0 48.1 jit_solution(15418099523693958545)
XLA Ops:
  0.6 46.4 %shard_map.148 = (bf16[2,256,1024]{2,1,0:T(8,128)(2,1)S(1)}, bf16[512,256]{1,0:T(8,128)(2,1)S(1)}, bf16[4,4,1024]{2,1,0:T(4,128)(2,1)S(1)}) custom-call(s32[64]{0:T(128)} %plen_ref.1, s32[4]{0:T(128)} %adm_ref.1, s32[4]{0:T(128)} %clen_ref.1, f32[1,128]{1,0:T(1,128)} %constant.2.clone.freq_ref, f32[1,128]{1,0:T(1,128)} %bitcast.8, f32[1,128]{1,0:T(1,128)} %bitcast.9, ...), custom_call_target="tpu_custom_call" | custom-call | flops 10499999744 | bytes 25000000 | tf_op jit(solution)/shard_map/pallas_call | solution.py:643
  47.1 1.1 %shard_map.149 = (bf16[2,256,1024]{2,1,0:T(8,128)(2,1)}, bf16[512,256]{1,0:T(8,128)(2,1)}, bf16[4,4,1024]{2,1,0:T(4,128)(2,1)}) custom-call(bf16[2,256,1024]{2,1,0:T(8,128)(2,1)S(1)} %get-tuple-element.9.out_v, bf16[512,256]{1,0:T(8,128)(2,1)S(1)} %get-tuple-element.10.hand_v, bf16[4,4,1024]{2,1,0:T(4,128)(2,1)S(1)} %get-tuple-element.11.dec_v), custom_call_target="tpu_custom_call" | custom-call | tf_op jit(solution)/shard_map/pallas_call | solution.py:712

commit v5 on v4

--- a/solution.py
+++ b/solution.py
@@ -104,8 +104,6 @@
     join_r,
     dpart_s,
     dpart_r,
-    out_v,
-    dout_v,
     small_sem,
     x_sem,
     in_sem,
@@ -577,12 +575,8 @@
         p, jj = i // 2, lax.rem(i, 2)
         for half in range(2):
             value = own_v[half, i] + part_r[2 + half, i].astype(F32)
-            out_v[half, i] = (value + part_r[4 + half, i].astype(F32)).astype(BF16)
-            pltpu.make_async_copy(
-                out_v.at[half, i],
-                out.at[p, half * HALF : (half + 1) * HALF, rows(jj * WIDE, WIDE)],
-                out_sem.at[2],
-            ).start()
+            value = (value + part_r[4 + half, i].astype(F32)).astype(BF16)
+            out[p, half * HALF : (half + 1) * HALF, rows(jj * WIDE, WIDE)] = value
         return carry
 
     def save_decoded():
@@ -591,8 +585,7 @@
             mine = join_r[pl.ds(8 * (b // 4) + b % 4, ROWS, stride=16), :]
             for t in range(STEPS):
                 one = mine[t * SLOTS : (t + 1) * SLOTS, :]
-                dout_v[t, :, b * HD : (b + 1) * HD] = one.astype(BF16)
-        pltpu.make_async_copy(dout_v, dec_out, out_sem.at[1]).start()
+                dec_out[t, :, b * HD : (b + 1) * HD] = one.astype(BF16)
 
     arrived(2, 0, 3)
     arrived(5, 0, 3)
@@ -605,8 +598,6 @@
     landed(dpart_s.at[1 : 2 * NH], dpart_ss.at[0])
     landed(join_r.at[0 : (NS - 1) * 8], seq_ss.at[2])
     landed(part_s, part_ss.at[0])
-    landed(out_v, out_sem.at[2])
-    landed(dout_v, out_sem.at[1])
 
 
 def store(out_v, hand_v, dec_v, out, handed, dec_out, sem):
@@ -638,13 +629,14 @@
     one = (THETA ** (-np.arange(half, dtype=np.float64) / half)).astype(np.float32)
     freq = jnp.asarray(np.concatenate([one, one])[None, :])
     hbm = pl.BlockSpec(memory_space=pl.ANY)
+    vmem = pl.BlockSpec(memory_space=pltpu.VMEM)
     dma = pltpu.SemaphoreType.DMA
     shapes = [(2, LP, WIDTH), (2 * LP, 2 * HD), (STEPS, SLOTS, WIDTH)]
     results = pl.pallas_call(
         kernel,
         out_shape=[pltpu.VMEM(shape, BF16) for shape in shapes],
         in_specs=[hbm] * 13,
-        out_specs=[hbm] * 3,
+        out_specs=[vmem, hbm, vmem],
         scratch_shapes=[
             pltpu.SMEM((2 * NS,), jnp.int32),
             pltpu.SMEM((SLOTS,), jnp.int32),
@@ -673,14 +665,12 @@
             pltpu.VMEM((NS * 8, HD), F32),
             pltpu.VMEM((2 * NH, 8, HD), F32),
             pltpu.VMEM((2 * NH, 8, HD), F32),
-            pltpu.VMEM((2, 4, HALF, WIDE), BF16),
-            pltpu.VMEM((STEPS, SLOTS, WIDTH), BF16),
             dma((4,)),
             dma((3,)),
             dma((2,)),
             dma((1 + NT,)),
             dma((4,)),
-            dma((3,)),
+            dma((1,)),
             dma((1,)),
             dma((9,)),
             dma((3,)),

time: 48.3 us -> 48.2 us (level)
  no operation moved by 1% of the time
where the time goes in v5:
time: 48.2 us; the launch traced here: 48.1 us
  Pallas kernels  47.4 us (98%)
  between operations  0.64 us (1%)
    pallas_call x1, Pallas kernels, local(): pl.pallas_call(kernel, out_shape=[pltpu.VMEM(shape, BF16) for shape in sh...  46.4 us
    pallas_call x1, Pallas kernels, local(): pl.pallas_call(store, out_shape=[jax.ShapeDtypeStruct(shape, BF16) for sh...  1.08 us

profile of v5, /device:TPU:1, one launch (start us, length us, event | category | flops | bytes accessed | tf_op | source)
XLA Modules:
  0.0 48.1 jit_solution(5505410920987531006)
XLA Ops:
  0.6 46.4 %shard_map.148 = (bf16[2,256,1024]{2,1,0:T(8,128)(2,1)S(1)}, bf16[512,256]{1,0:T(8,128)(2,1)S(1)}, bf16[4,4,1024]{2,1,0:T(4,128)(2,1)S(1)}) custom-call(s32[64]{0:T(128)} %plen_ref.1, s32[4]{0:T(128)} %adm_ref.1, s32[4]{0:T(128)} %clen_ref.1, f32[1,128]{1,0:T(1,128)} %constant.2.clone.freq_ref, f32[1,128]{1,0:T(1,128)} %bitcast.8, f32[1,128]{1,0:T(1,128)} %bitcast.9, ...), custom_call_target="tpu_custom_call" | custom-call | flops 10499999744 | bytes 25000000 | tf_op jit(solution)/shard_map/pallas_call | solution.py:635
  47.0 1.1 %shard_map.149 = (bf16[2,256,1024]{2,1,0:T(8,128)(2,1)}, bf16[512,256]{1,0:T(8,128)(2,1)}, bf16[4,4,1024]{2,1,0:T(4,128)(2,1)}) custom-call(bf16[2,256,1024]{2,1,0:T(8,128)(2,1)S(1)} %get-tuple-element.9.out_v, bf16[512,256]{1,0:T(8,128)(2,1)S(1)} %get-tuple-element.10.hand_v, bf16[4,4,1024]{2,1,0:T(4,128)(2,1)S(1)} %get-tuple-element.11.dec_v), custom_call_target="tpu_custom_call" | custom-call | tf_op jit(solution)/shard_map/pallas_call | solution.py:702

commit v6 on v5

--- a/solution.py
+++ b/solution.py
@@ -20,6 +20,8 @@
 CACHE = 512
 NS = 32
 NH = 4
+NX = 4
+PER_X = NS // NX
 EACH = LP // NS
 EPS = 1e-06
 THETA = 1000000.0
@@ -116,6 +118,7 @@
     seq_rs,
     dpart_ss,
     dpart_rs,
+    row_sem,
 ):
     y = lax.axis_index("head")
     me = lax.axis_index("seq")
@@ -178,23 +181,18 @@
 
     barrier = pltpu.get_barrier_semaphore()
 
-    def greet(i, carry):
-        pl.semaphore_signal(
-            barrier,
-            inc=1,
-            device_id={"seq": lax.rem(me + i, NS)},
-            device_id_type=pl.DeviceIdType.MESH,
-        )
-        return carry
+    def signal(sem, **where):
+        pl.semaphore_signal(sem, inc=1, device_id=where, device_id_type=pl.DeviceIdType.MESH)
+
+    def signal_x(sem):
+        for i in range(1, NX):
+            signal(sem, seq=lax.rem(me + i * PER_X, NS))
 
     for k in range(1, NH):
-        pl.semaphore_signal(
-            barrier,
-            inc=1,
-            device_id={"head": lax.rem(y + k, NH)},
-            device_id_type=pl.DeviceIdType.MESH,
-        )
-    lax.fori_loop(1, NS, greet, 0)
+        signal(barrier, head=lax.rem(y + k, NH))
+    signal_x(barrier)
+    for i in range(1, PER_X):
+        signal(barrier, seq=me - lax.rem(me, PER_X) + lax.rem(me + i, PER_X))
 
     load_q(2).start()
 
@@ -291,7 +289,14 @@
             pa_v[half, rows(p * HALF, HALF), head * HD : (head + 1) * HD] = one
 
     def arrival(slot, i):
-        return {0: 0, 1: 1 + i // 3, 2: 3 + i // 3, 5: 5 + i // 3, 3: 7, 4: 8}[slot]
+        return {
+            0: (i + 2) // 3,
+            1: 2 + (i + 1) // 2,
+            2: 5 + i // 3,
+            5: 7 + i // 3,
+            3: 9,
+            4: 10,
+        }[slot]
 
     def arrived(slot, first, last):
         landed(part_r.at[slot, first:last], part_rs.at[arrival(slot, first)])
@@ -334,7 +339,7 @@
 
                 @pl.when(jj == 0)
                 def _():
-                    pl.semaphore_wait(barrier, NS - 1 + NH - 1)
+                    pl.semaphore_wait(barrier, NH - 1 + NX - 1 + PER_X - 1)
 
             send(0, ((2, 0), (3, 4)), p, jj)
             return carry
@@ -343,6 +348,7 @@
 
         @pl.when(p == 0)
         def _():
+            signal_x(row_sem)
             load_dec.start()
             load_x(1, 0).start()
             load_x(1, 1).start()
@@ -414,11 +420,34 @@
             hand(i, me).start()
             return carry
 
+        pl.semaphore_wait(row_sem, NX - 1)
         lax.fori_loop(1, NS, hand_start, 0)
 
     multiply_second(hand_over)
     landed(wo_v.at[1], wo_sem.at[3])
+    def mixed_right(i):
+        send(0, ((1, 2),), i // 2, lax.rem(i, 2), 0)
+
+    def mixed_left(i):
+        send(1, ((3, 5),), i // 2, lax.rem(i, 2), 1)
+
+    def mixed_rows(half, k, slot, far, start):
+        some = pl.ds(start, HALF // 2)
+        mine = pa_v[half, some, :]
+        value = jnp.concatenate([dot(mine, wo_v[k, b]) for b in range(2)], axis=1)
+        value = value + part_r[far, 0, some, :].astype(F32)
+        part_s[slot, 0, some, :] = value.astype(BF16)
+        remote(
+            part_s.at[slot, 0, some],
+            part_r.at[slot, 0, some],
+            part_ss.at[0],
+            part_rs.at[arrival(slot, 0)],
+            head=right if slot == 2 else left,
+        ).start()
+
     second_half(0)
+    arrived(0, 0, 1)
+    mixed_rows(0, 1, 2, 0, 0)
     load_cache.wait()
 
     landed(hand_v.at[0 : (NS - 1) * 16], seq_rs.at[0])
@@ -497,6 +526,9 @@
 
     lax.fori_loop(0, 4, own, 0)
 
+    arrived(1, 0, 1)
+    mixed_rows(1, 3, 5, 1, 0)
+
     landed(soft_r.at[0 : (NS - 1) * 8], seq_rs.at[1])
     joined = []
     for q in range(heads // NS):
@@ -535,17 +567,19 @@
             if (k, e) != (0, 0):
                 dpart(k, e).start()
 
-    arrived(0, 0, 4)
-    arrived(1, 0, 3)
-
-    def mixed(i, carry):
-        send(0, ((1, 2),), i // 2, lax.rem(i, 2), 0)
-        send(1, ((3, 5),), i // 2, lax.rem(i, 2), 1)
+    def right_tile(i, carry):
+        mixed_right(i)
         return carry
 
-    lax.fori_loop(0, 3, mixed, 0)
+    mixed_rows(0, 1, 2, 0, HALF // 2)
+    mixed_rows(1, 3, 5, 1, HALF // 2)
+    arrived(0, 1, 4)
+    lax.fori_loop(1, 4, right_tile, 0)
+    arrived(1, 1, 3)
+    for i in (1, 2):
+        mixed_left(i)
     arrived(1, 3, 4)
-    mixed(3, 0)
+    mixed_left(3)
 
     landed(dpart_r.at[1 : 2 * NH], dpart_rs.at[0])
     total = dpart_s[0]
@@ -672,11 +706,12 @@
             dma((4,)),
             dma((1,)),
             dma((1,)),
-            dma((9,)),
+            dma((11,)),
             dma((3,)),
             dma((3,)),
             dma((1,)),
             dma((1,)),
+            pltpu.SemaphoreType.REGULAR,
         ],
         compiler_params=pltpu.CompilerParams(
             collective_id=0, has_side_effects=True, vmem_limit_bytes=56 * 2**20

time: 48.2 us -> 47 us (0.975)
  Pallas kernels: 47.4 us -> 46.2 us
    pallas_call x1, Pallas kernels: 46.4 us -> 45.2 us  [local(): pl.pallas_call(kernel, out_shape=[pltpu.VMEM(shape, BF16) for shape in sh...]
where the time goes in v6:
time: 47 us; the launch traced here: 46.9 us
  Pallas kernels  46.2 us (98%)
  between operations  0.64 us (1%)
    pallas_call x1, Pallas kernels, local(): pl.pallas_call(kernel, out_shape=[pltpu.VMEM(shape, BF16) for shape in sh...  45.2 us
    pallas_call x1, Pallas kernels, local(): pl.pallas_call(store, out_shape=[jax.ShapeDtypeStruct(shape, BF16) for sh...  1.08 us

profile of v6, /device:TPU:1, one launch (start us, length us, event | category | flops | bytes accessed | tf_op | source)
XLA Modules:
  0.0 46.9 jit_solution(11463009429254752943)
XLA Ops:
  0.6 45.2 %shard_map.148 = (bf16[2,256,1024]{2,1,0:T(8,128)(2,1)S(1)}, bf16[512,256]{1,0:T(8,128)(2,1)S(1)}, bf16[4,4,1024]{2,1,0:T(4,128)(2,1)S(1)}) custom-call(s32[64]{0:T(128)} %plen_ref.1, s32[4]{0:T(128)} %adm_ref.1, s32[4]{0:T(128)} %clen_ref.1, f32[1,128]{1,0:T(1,128)} %constant.2.clone.freq_ref, f32[1,128]{1,0:T(1,128)} %bitcast.8, f32[1,128]{1,0:T(1,128)} %bitcast.9, ...), custom_call_target="tpu_custom_call" | custom-call | flops 10499999744 | bytes 25000000 | tf_op jit(solution)/shard_map/pallas_call | solution.py:669
  45.8 1.1 %shard_map.149 = (bf16[2,256,1024]{2,1,0:T(8,128)(2,1)}, bf16[512,256]{1,0:T(8,128)(2,1)}, bf16[4,4,1024]{2,1,0:T(4,128)(2,1)}) custom-call(bf16[2,256,1024]{2,1,0:T(8,128)(2,1)S(1)} %get-tuple-element.9.out_v, bf16[512,256]{1,0:T(8,128)(2,1)S(1)} %get-tuple-element.10.hand_v, bf16[4,4,1024]{2,1,0:T(4,128)(2,1)S(1)} %get-tuple-element.11.dec_v), custom_call_target="tpu_custom_call" | custom-call | tf_op jit(solution)/shard_map/pallas_call | solution.py:737

commit v7 on v6

--- a/solution.py
+++ b/solution.py
@@ -248,13 +248,16 @@
                 def _():
                     load_x(0, 1).start()
 
+            @pl.when(t == 2)
+            def _():
+                keys_values(0, p, 0)
+
             finish_query(0, p, lax.rem(t + 5, 6), 0)
             f_v[t, 0:HALF, :] = dot(x_v[rows(p * HALF, HALF), :], w_v[t])
             return carry
 
         lax.fori_loop(0, 1 + NT, tile, 0)
         finish_query(0, p, NT, 0)
-        keys_values(0, p, 0)
 
     def multiply_second(after_keys):
         def finish(t):
@@ -605,12 +608,19 @@
     arrived(3, 0, 4)
     arrived(4, 0, 4)
 
+    def early(i, carry):
+        own_v[0, i] = own_v[0, i] + part_r[4, i].astype(F32)
+        own_v[1, i] = own_v[1, i] + part_r[3, i].astype(F32)
+        return carry
+
+    lax.fori_loop(0, 4, early, 0)
+
     def finish(i, carry):
         p, jj = i // 2, lax.rem(i, 2)
         for half in range(2):
-            value = own_v[half, i] + part_r[2 + half, i].astype(F32)
-            value = (value + part_r[4 + half, i].astype(F32)).astype(BF16)
-            out[p, half * HALF : (half + 1) * HALF, rows(jj * WIDE, WIDE)] = value
+            value = own_v[half, i] + part_r[5 if half else 2, i].astype(F32)
+            at = pl.ds(half * HALF, HALF)
+            out[p, at, rows(jj * WIDE, WIDE)] = value.astype(BF16)
         return carry
 
     def save_decoded():

time: 47 us -> 47 us (level)
  no operation moved by 1% of the time
where the time goes in v7:
time: 47 us; the launch traced here: 46.9 us
  Pallas kernels  46.2 us (98%)
  between operations  0.64 us (1%)
    pallas_call x1, Pallas kernels, local(): pl.pallas_call(kernel, out_shape=[pltpu.VMEM(shape, BF16) for shape in sh...  45.1 us
    pallas_call x1, Pallas kernels, local(): pl.pallas_call(store, out_shape=[jax.ShapeDtypeStruct(shape, BF16) for sh...  1.08 us

profile of v7, /device:TPU:1, one launch (start us, length us, event | category | flops | bytes accessed | tf_op | source)
XLA Modules:
  0.0 46.9 jit_solution(10670959063543543502)
XLA Ops:
  0.6 45.1 %shard_map.148 = (bf16[2,256,1024]{2,1,0:T(8,128)(2,1)S(1)}, bf16[512,256]{1,0:T(8,128)(2,1)S(1)}, bf16[4,4,1024]{2,1,0:T(4,128)(2,1)S(1)}) custom-call(s32[64]{0:T(128)} %plen_ref.1, s32[4]{0:T(128)} %adm_ref.1, s32[4]{0:T(128)} %clen_ref.1, f32[1,128]{1,0:T(1,128)} %constant.2.clone.freq_ref, f32[1,128]{1,0:T(1,128)} %bitcast.8, f32[1,128]{1,0:T(1,128)} %bitcast.9, ...), custom_call_target="tpu_custom_call" | custom-call | flops 10499999744 | bytes 25000000 | tf_op jit(solution)/shard_map/pallas_call | solution.py:679
  45.8 1.1 %shard_map.149 = (bf16[2,256,1024]{2,1,0:T(8,128)(2,1)}, bf16[512,256]{1,0:T(8,128)(2,1)}, bf16[4,4,1024]{2,1,0:T(4,128)(2,1)}) custom-call(bf16[2,256,1024]{2,1,0:T(8,128)(2,1)S(1)} %get-tuple-element.9.out_v, bf16[512,256]{1,0:T(8,128)(2,1)S(1)} %get-tuple-element.10.hand_v, bf16[4,4,1024]{2,1,0:T(4,128)(2,1)S(1)} %get-tuple-element.11.dec_v), custom_call_target="tpu_custom_call" | custom-call | tf_op jit(solution)/shard_map/pallas_call | solution.py:747

commit v8 on v7

--- a/solution.py
+++ b/solution.py
@@ -93,6 +93,8 @@
     kv_v,
     give_v,
     hand_v,
+    mask_v,
+    turned_v,
     q_v,
     dq_v,
     dkv_v,
@@ -226,6 +228,16 @@
         kv_v[to, 0:HD] = normrot(mine[:, 0:HD], tab_v[half, 2], tab_v[half, 3]).astype(BF16)
         kv_v[to, HD : 2 * HD] = mine[:, HD : 2 * HD].astype(BF16)
 
+    def bias_of(half, p):
+        keys = (half + 1) * HALF
+        at = iota((keys, HALF), 0)
+        causal = at <= iota((keys, HALF), 1) + half * HALF
+        return jnp.where(causal & (at < plen[2 * me + p]), 0.0, NEG)
+
+    def turned(half, p):
+        mine = pl.ds(pl.multiple_of(p * LP, LP), (half + 1) * HALF)
+        return kv_v[mine, HD : 2 * HD].astype(F32).T.astype(BF16)
+
     def multiply_first(p):
         def tile(t, carry):
             @pl.when(p == 0)
@@ -252,6 +264,11 @@
             def _():
                 keys_values(0, p, 0)
 
+            @pl.when(t == 3)
+            def _():
+                mask_v[...] = bias_of(0, p)
+                turned_v[...] = turned(0, p)
+
             finish_query(0, p, lax.rem(t + 5, 6), 0)
             f_v[t, 0:HALF, :] = dot(x_v[rows(p * HALF, HALF), :], w_v[t])
             return carry
@@ -276,16 +293,14 @@
 
     def attend(half, p):
         keys = (half + 1) * HALF
-        at = iota((keys, HALF), 0)
-        causal = at <= iota((keys, HALF), 1) + half * HALF
-        bias = jnp.where(causal & (at < plen[2 * me + p]), 0.0, NEG)
         mine = rows(p * LP, keys) if half else pl.ds(pl.multiple_of(p * LP, LP), keys)
+        bias = bias_of(1, p) if half else mask_v[...]
         scores = dot_nt(kv_v[mine, 0:HD], q_v[p, 0 : GROUP * HALF])
         scores = scores + jnp.concatenate([bias] * GROUP, axis=1)
         top = jnp.max(scores, axis=0, keepdims=True)
         expo = jnp.exp2((scores - top) * (SCALE * LOG2E))
         weights = expo * (1.0 / jnp.sum(expo, axis=0, keepdims=True))
-        values = kv_v[mine, HD : 2 * HD].astype(F32).T.astype(BF16)
+        values = turned(1, p) if half else turned_v[...]
         mixed = dot(values, weights.astype(BF16))
         for head in range(GROUP):
             one = mixed[:, head * HALF : (head + 1) * HALF].T.astype(BF16)
@@ -696,6 +711,8 @@
             pltpu.VMEM((2 * LP, 2 * HD), BF16),
             pltpu.VMEM((2 * LP, 2 * HD), BF16),
             pltpu.VMEM((2 * LP, 2 * HD), BF16),
+            pltpu.VMEM((HALF, HALF), F32),
+            pltpu.VMEM((HD, HALF), BF16),
             pltpu.VMEM((2, (GROUP + 4) * HALF, HD), BF16),
             pltpu.VMEM(((GROUP + 4) * ROWS, HD), BF16),
             pltpu.VMEM((HD, 2 * HD), BF16),

time: 47 us -> 47.1 us (level)
  no operation moved by 1% of the time
where the time goes in v8:
time: 47.1 us; the launch traced here: 47 us
  Pallas kernels  46.3 us (98%)
  between operations  0.64 us (1%)
    pallas_call x1, Pallas kernels, local(): pl.pallas_call(kernel, out_shape=[pltpu.VMEM(shape, BF16) for shape in sh...  45.3 us
    pallas_call x1, Pallas kernels, local(): pl.pallas_call(store, out_shape=[jax.ShapeDtypeStruct(shape, BF16) for sh...  1.08 us

profile of v8, /device:TPU:1, one launch (start us, length us, event | category | flops | bytes accessed | tf_op | source)
XLA Modules:
  0.0 47.0 jit_solution(17785722692237723251)
XLA Ops:
  0.6 45.3 %shard_map.148 = (bf16[2,256,1024]{2,1,0:T(8,128)(2,1)S(1)}, bf16[512,256]{1,0:T(8,128)(2,1)S(1)}, bf16[4,4,1024]{2,1,0:T(4,128)(2,1)S(1)}) custom-call(s32[64]{0:T(128)} %plen_ref.1, s32[4]{0:T(128)} %adm_ref.1, s32[4]{0:T(128)} %clen_ref.1, f32[1,128]{1,0:T(1,128)} %constant.2.clone.freq_ref, f32[1,128]{1,0:T(1,128)} %bitcast.8, f32[1,128]{1,0:T(1,128)} %bitcast.9, ...), custom_call_target="tpu_custom_call" | custom-call | flops 10499999744 | bytes 25000000 | tf_op jit(solution)/shard_map/pallas_call | solution.py:694
  45.9 1.1 %shard_map.149 = (bf16[2,256,1024]{2,1,0:T(8,128)(2,1)}, bf16[512,256]{1,0:T(8,128)(2,1)}, bf16[4,4,1024]{2,1,0:T(4,128)(2,1)}) custom-call(bf16[2,256,1024]{2,1,0:T(8,128)(2,1)S(1)} %get-tuple-element.9.out_v, bf16[512,256]{1,0:T(8,128)(2,1)S(1)} %get-tuple-element.10.hand_v, bf16[4,4,1024]{2,1,0:T(4,128)(2,1)S(1)} %get-tuple-element.11.dec_v), custom_call_target="tpu_custom_call" | custom-call | tf_op jit(solution)/shard_map/pallas_call | solution.py:764
